TPU v7x, 256 devices: a whole 4x4x8 slice. The times are simulated.
256 devices in a mesh: wide: 32 (over y, z_lo, core), narrow: 8 (over x, z_hi).
Axes of the slice: x: 4, y: 4, z: 8 (z_hi: 2, z_lo: 4; z = z_hi * 4 + z_lo), core: 2. Of those that a mesh axis runs over, the one named last changes fastest.
Arguments:
- amplitudes: bfloat16 [524288, 1024], P(('wide', 'narrow')), may hold values from -0.03125 to 0.03125
- integral_slab: bfloat16 [524288, 1024], P(('wide', 'narrow')), may hold values from -0.046875 to 0.046875
- coupling: float32 [256, 1024, 1024], P(('wide', 'narrow')), may hold values from -0.046875 to 0.046875
- pair_of_block: int32 [256], replicated, may hold values from 0 to 255, each once
- pair_shift: float32 [256], replicated, may hold values from -4 to 4
- virt_energy: float32 [1024], replicated, may hold values from 0 to 26
- core_energy: float32 [64], replicated, may hold values from -6 to -4
- core_index: int32 [2], replicated, may hold values from 0 to 63, as said below
- frequency: float32 [16], replicated, may hold values from 6 to 30
- dipole: float32 [64, 1024], P(None, 'narrow'), may hold values from -6 to 6
Outputs:
- response: float32 [2, 32, 1024], P(None, None, 'narrow')
- residual_rms: float32 [2, 32], replicated
Inputs may be any that keep to these rules, and one draw needn't show every extreme that they name: `core_index`: the 2 core orbitals are different occupied orbitals, and the last of them is orbital 64 - 1.
All inputs are finite; a program needn't handle non-finite values.
Results may differ from a plain program's by a relative error of at most 0.0003.
Values sent between devices are 32-bit elements; how exact they have to be, the bound alone decides.
A program may use at most 64 MiB of HBM per device.

v0:
```python
from functools import partial

import jax
import jax.numpy as jnp
from jax import lax
from jax.sharding import PartitionSpec as P

ITERS = 2


damping = 0.5
highest = lax.Precision.HIGHEST
contract_rows = (((0,), (0,)), ((), ()))
contract_last = (((1,), (1,)), ((), ()))
contract_pairs = (((0, 2), (0, 1)), ((), ()))


def divide_precond(real_part, imag_part, level, level_mag):
    return (
        (real_part * level - imag_part * damping) / level_mag,
        (imag_part * level + real_part * damping) / level_mag,
    )


def divide_denom(real_part, imag_part, denom_real, denom_mag):
    return (
        (real_part * denom_real + imag_part * damping) / denom_mag,
        (imag_part * denom_real - real_part * damping) / denom_mag,
    )


def apply_precond(real_part, imag_part, level):
    return (level * real_part + damping * imag_part, level * imag_part - damping * real_part)


def side_singles(singles, total, flattened, start):
    return lax.dot_general(
        flattened, singles, contract_last, precision=highest, preferred_element_type=jnp.float32
    )


def absorb(coupling, side, carry, piece, start):
    doubles_in, side_total = carry
    width = piece.shape[2]
    flattened = piece.reshape(-1, width)
    columns = coupling[0]
    updates = [
        lax.dot_general(
            flattened, columns, contract_last, precision=highest, preferred_element_type=jnp.float32
        )
    ]
    doubles_in = jnp.stack(updates, 0)
    side_total = side(side_total, flattened, start)
    return (doubles_in, side_total)


def per_device(
    amplitudes,
    integral_slab,
    coupling,
    pair_of_block,
    pair_shift,
    virt_energy,
    core_energy,
    core_index,
    frequency,
    dipole,
):
    virt_total = virt_energy.shape[0]
    block_rows = dipole.shape[1]
    row_start = lax.axis_index("narrow") * block_rows
    freq_count = frequency.shape[0]
    mode_count = freq_count * core_index.shape[0]
    local_pairs = coupling.shape[0]
    pair_count = pair_of_block.shape[0]
    chooser = (
        core_index[:, None] == jnp.arange(core_energy.shape[0], dtype=jnp.int32)[None, :]
    ).astype(jnp.float32)
    picked_energy = jnp.sum(chooser * core_energy[None, :], axis=1)
    picked_dipole = jnp.dot(chooser, dipole, precision=highest)
    shift = (frequency[None, :] + picked_energy[:, None]).reshape(-1)
    level = lax.dynamic_slice_in_dim(virt_energy, row_start, block_rows)[None, :] - shift[:, None]
    level_mag = level * level + damping * damping
    rhs = jnp.repeat(picked_dipole, freq_count, axis=0)
    slot_ids = lax.axis_index(("wide", "narrow")) * local_pairs + jnp.arange(
        local_pairs, dtype=jnp.int32
    )
    slot_match = slot_ids[:, None] == jnp.arange(pair_count, dtype=jnp.int32)[None, :]
    pair_ids = jnp.sum(jnp.where(slot_match, pair_of_block[None, :], 0), axis=1)
    pair_match = pair_ids[:, None] == jnp.arange(pair_count, dtype=jnp.int32)[None, :]
    slot_shift = jnp.sum(jnp.where(pair_match, pair_shift[None, :], 0.0), axis=1)
    denom_real = shift[None, :, None] - slot_shift[:, None, None] - virt_energy[None, None, :]
    denom_mag = denom_real * denom_real + damping * damping
    empty_singles = jnp.zeros((2 * mode_count, block_rows), jnp.float32)
    whole = lax.dot_general(
        amplitudes, integral_slab, contract_rows, preferred_element_type=jnp.float32
    )
    whole = lax.psum(whole, ("wide", "narrow"))
    singles = lax.dynamic_slice_in_dim(whole, row_start, block_rows, 0)
    side = partial(side_singles, singles)
    resp_re, resp_im = divide_precond(rhs, jnp.zeros_like(rhs), level, level_mag)
    empty_doubles = jnp.zeros((local_pairs, 2 * mode_count, virt_total), jnp.float32)
    fold_plain = partial(absorb, coupling, side)
    rms_rows = []
    for sweep in range(ITERS):
        response = jnp.stack([resp_re, resp_im], 0)
        if sweep == 0:
            doubles_in, singles_term = fold_plain(
                (empty_doubles, empty_singles),
                lax.all_gather(response, "narrow", axis=2, tiled=True),
                jnp.int32(0),
            )
        else:
            doubles_in, singles_term = fold_plain(
                (empty_doubles, empty_singles),
                lax.all_gather(response, "narrow", axis=2, tiled=True),
                jnp.int32(0),
            )
        out_re, out_im = divide_denom(
            doubles_in[:, :mode_count], doubles_in[:, mode_count:], denom_real, denom_mag
        )
        outgoing = jnp.concatenate([out_re, out_im], 1)
        folded = lax.dot_general(
            outgoing,
            coupling,
            contract_pairs,
            precision=highest,
            preferred_element_type=jnp.float32,
        )
        summed = lax.psum(folded, ("wide", "narrow"))
        summed = lax.dynamic_slice_in_dim(summed, row_start, block_rows, 1)
        applied = summed + singles_term
        app_re, app_im = apply_precond(resp_re, resp_im, level)
        res_re = rhs - (app_re + applied[:mode_count])
        res_im = -(app_im + applied[mode_count:])
        partial_squares = jnp.sum(res_re * res_re + res_im * res_im, axis=1)
        total_squares = lax.psum(partial_squares, "narrow")
        rms_rows.append(jnp.sqrt(total_squares / (2 * virt_total) + 1e-06))
        step_re, step_im = divide_precond(res_re, res_im, level, level_mag)
        resp_re = resp_re + step_re
        resp_im = resp_im + step_im
    return (jnp.stack([resp_re, resp_im], 0), jnp.stack(rms_rows, 0))


def solution(mesh):
    placed = (
        P(("wide", "narrow"), None),
        P(("wide", "narrow"), None),
        P(("wide", "narrow"), None, None),
        P(),
        P(),
        P(),
        P(),
        P(),
        P(),
        P(None, "narrow"),
    )
    return jax.shard_map(
        per_device,
        mesh=mesh,
        in_specs=placed,
        out_specs=(P(None, None, "narrow"), P()),
        check_vma=False,
    )
```

profile of v0, /device:TPU:1, one launch (start us, length us, event | category | flops | bytes accessed | tf_op | source)
XLA Modules:
  0.0 693.0 jit_solution(18028242555270349725)
XLA Ops:
  7.2 0.0 copy-start
  7.2 0.0 copy-start.3
  7.2 0.0 all-reduce.7.cloned.1.call-start
  7.2 0.9 select_reduce_fusion
  8.1 0.7 broadcast_add_fusion
  8.8 0.1 add.155
  8.9 0.0 copy-done
  8.9 0.8 fusion.61
  9.8 0.0 copy-start.1
  9.8 1.5 fusion.59
  11.2 1.9 fusion.60
  13.2 0.8 dynamic_slice.12
  13.9 0.6 broadcast_subtract_fusion
  14.6 0.1 fusion.31
  14.7 41.1 %all_gather.6 = f32[2,32,1024]{2,1,0:T(8,128)S(1)} all-gather(f32[2,32,128]{2,1,0:T(8,128)S(1)} %pad_maximum_fusion), channel_id=1, replica_groups=mesh['wide'=32,'narrow'=8] {'narrow'}, dimensions={2}, use_global_device_ids=true | all-gather | bytes 294912 | tf_op jit(solution)/shard_map/all_gather | solution.py:110
  55.8 0.0 copy-start.4
  55.8 6.4 fusion.8
  62.2 0.0 copy-done.3
  62.2 0.1 fusion.21
  62.3 0.0 copy-done.1
  62.3 3.4 fusion.4
  65.7 0.0 copy-done.4
  65.7 8.4 %fusion.68 = f32[1024,1024]{1,0:T(8,128)} fusion(bf16[2048,1024]{1,0:T(8,128)(2,1)S(1)} %copy-done.4, bf16[2048,1024]{1,0:T(8,128)(2,1)} %param.11), kind=kOutput, calls=%fused_computation.104 | convolution fusion | flops 4294967296 | bytes 12582912 | tf_op jit(solution)/shard_map/dot_general | solution.py:95
  74.1 0.0 all-reduce.7.cloned.1.call-update
  74.1 0.0 all-reduce.5.cloned.1.call-start
  74.1 276.0 %all-reduce.7.cloned.1.call-done = (f32[1024,1024]{1,0:T(8,128)}, f32[64,1024]{1,0:T(8,128)}) async-done(((f32[1024,1024]{1,0:T(8,128)}, f32[64,1024]{1,0:T(8,128)}), (f32[1024,1024]{1,0:T(8,128)}, f32[64,1024]{1,0:T(8,128)})) %all-reduce.7.cloned.1.call-update) | async-done | bytes 4456464 | tf_op jit(solution)/shard_map/psum | solution.py:98
  350.2 0.0 copy-start.2
  350.2 1.9 convolution_add_fusion.1
  352.0 0.2 add_reduce_fusion.1
  352.2 0.1 fusion.41
  352.3 38.3 %all_gather.7 = f32[2,32,1024]{2,1,0:T(8,128)S(1)} all-gather(f32[2,32,128]{2,1,0:T(8,128)S(1)} %pad_maximum_fusion.1), channel_id=1, replica_groups=mesh['wide'=32,'narrow'=8] {'narrow'}, dimensions={2}, use_global_device_ids=true | all-gather | bytes 294912 | tf_op jit(solution)/shard_map/all_gather | solution.py:116
  390.7 6.2 fusion.11
  396.9 0.1 fusion.24
  397.1 0.0 copy-done.2
  397.1 3.3 fusion
  400.4 0.0 all-reduce.5.cloned.1.call-update
  400.4 255.4 %all-reduce.5.cloned.1.call-done = f32[64,1024]{1,0:T(8,128)} async-done(((f32[64,1024]{1,0:T(8,128)}), f32[64,1024]{1,0:T(8,128)}) %all-reduce.5.cloned.1.call-update) | async-done | bytes 262160 | tf_op jit(solution)/shard_map/psum | solution.py:130
  655.9 1.7 convolution_add_fusion
  657.6 0.2 add_reduce_fusion
  657.8 0.1 fusion.44
  657.9 0.6 pad_maximum_fusion.2
  658.5 27.1 %all-reduce.1 = (f32[32]{0:T(128)S(1)}, f32[32]{0:T(128)S(1)}) all-reduce(f32[32]{0:T(128)S(1)} %get-tuple-element.9, f32[32]{0:T(128)S(1)} %get-tuple-element.6), channel_id=1, replica_groups=mesh['wide'=32,'narrow'=8] {'narrow'}, use_global_device_ids=true, to_apply=%region_9.10 | all-reduce | flops 64 | bytes 512 | tf_op jit(solution)/shard_map/psum | solution.py:137
  685.6 0.6 pad_maximum_fusion.3
  (4 shorter events, 0.0 us)
Async XLA Ops:
  7.2 1.8 copy-start
  7.2 55.0 %copy-start.3 = (f32[1024]{0:T(1024)S(1)}, f32[1024]{0:T(1024)}, u32[]{:S(2)}) copy-start(f32[1024]{0:T(1024)} %param.15) | copy-start | bytes 12292
  7.2 343.0 %all-reduce.7.cloned.1.call-start = ((), (), s32[]{:S(2)}) async-start(), calls=%async_computation.1 | async-start | bytes 8912896 | tf_op jit(solution)/shard_map/psum | solution.py:98
  9.8 52.6 %copy-start.1 = (f32[1,1024,1024]{2,1,0:T(8,128)S(1)}, f32[1,1024,1024]{2,1,0:T(8,128)}, u32[]{:S(2)}) copy-start(f32[1,1024,1024]{2,1,0:T(8,128)} %param.12) | copy-start | bytes 12582916
  55.8 9.9 %copy-start.4 = (bf16[2048,1024]{1,0:T(8,128)(2,1)S(1)}, bf16[2048,1024]{1,0:T(8,128)(2,1)}, u32[]{:S(2)}) copy-start(bf16[2048,1024]{1,0:T(8,128)(2,1)} %param.10) | copy-start | bytes 12582916
  74.1 581.8 %all-reduce.5.cloned.1.call-start = ((), (), s32[]{:S(2)}) async-start(), calls=%async_computation | async-start | bytes 524288 | tf_op jit(solution)/shard_map/psum | solution.py:130
  350.2 46.9 %copy-start.2 = (f32[1,1024,1024]{2,1,0:T(8,128)S(1)}, f32[1,1024,1024]{2,1,0:T(8,128)}, u32[]{:S(2)}) copy-start(f32[1,1024,1024]{2,1,0:T(8,128)} %param.12) | copy-start | bytes 12582916
Sparse Core Ops, SparseCore 0:
  74.2 275.9 all-reduce.6
  400.6 255.2 all-reduce.4
where the time goes:
time: 696 us; the launch traced here: 693 us
  waiting for transfers between devices  531 us (76%)
  blocking collectives  107 us (15%)
  matrix products  32.1 us (5%)
  between operations  14.2 us (2%)
  other arithmetic  7.74 us (1%)
    psum x1, waiting for transfers between devices, per_device(): whole = lax.psum(whole, ('wide', 'narrow'))  276 us
    psum x1, waiting for transfers between devices, per_device(): summed = lax.psum(folded, ('wide', 'narrow'))  255 us
    all_gather x2, blocking collectives, per_device(): lax.all_gather(response, 'narrow', axis=2, tiled=True)  79.5 us
    psum x1, blocking collectives, per_device(): total_squares = lax.psum(partial_squares, 'narrow')  27.1 us
  transfers between devices with their start and end apart: 2, of which 2 were waited for; matrix products, arithmetic and copies ran while one was open for 0% of the time, Pallas kernels for 0%

commit v1 on v0

v1 whole, which is shorter than its diff:
```python
from functools import partial

import jax
import jax.numpy as jnp
from jax import lax
from jax.experimental import pallas as pl
from jax.experimental.pallas import tpu as pltpu
from jax.sharding import PartitionSpec as P

ITERS = 2
DAMP = 0.5
MESH = pl.DeviceIdType.MESH
F32 = jnp.float32
BF16 = jnp.bfloat16

NX, NY, NZ, NZLO = 4, 4, 8, 4
PLANE = tuple((dx, dy) for dx in range(NX) for dy in range(NY))[1:]
GROUPS, SUB, LANES, BLOCKS = 4, 8, 128, 8
PIECE = 2 * SUB
COLS = GROUPS * PIECE
HALF = BLOCKS // 2


def place(x, y, z, core):
    return {
        "wide": (y * NZLO + lax.rem(z, NZLO)) * 2 + core,
        "narrow": x * 2 + z // NZLO,
    }


def nt(left, right):
    return lax.dot_general(left, right, (((1,), (1,)), ((), ())), preferred_element_type=F32)


def nn(left, right):
    return lax.dot_general(left, right, (((1,), (0,)), ((), ())), preferred_element_type=F32)


def halves(value):
    high = value.astype(BF16)
    low = (value - high.astype(F32)).astype(BF16)
    return high, low


def kernel(
    pair_of_block, pair_shift, core_energy, core_index, frequency,
    virt, dipole, amp_hbm, slab_hbm, coup_hbm,
    out_ref, rms_ref,
    amp, slab, coup, coup_hi, coup_lo,
    picked, dip, rhs, pre_re, pre_im, level, den_re, den_im, resp, pieces, t_pieces, w_pieces,
    part, from_core, own, from_plane, columns, applied, spare,
    hbm_sem, dip_sems, core_sems, plane_sems, column_sems, gather_sems, share_sems,
):
    wide, narrow = lax.axis_index("wide"), lax.axis_index("narrow")
    x, y, core = narrow // 2, wide // (2 * NZLO), lax.rem(wide, 2)
    z_hi, z_lo = lax.rem(narrow, 2), lax.rem(wide // 2, NZLO)
    z = z_hi * NZLO + z_lo
    mirror = (1 - z_hi) * NZLO + lax.rem(z_lo + 2, NZLO)

    loads = [
        pltpu.make_async_copy(slab_hbm, slab, hbm_sem.at[0]),
        pltpu.make_async_copy(coup_hbm.at[0], coup, hbm_sem.at[1]),
        pltpu.make_async_copy(amp_hbm, amp, hbm_sem.at[2]),
    ]
    for load in loads:
        load.start()

    sibling = place(x, y, z, 1 - core)
    plane = [place(lax.rem(x + dx, NX), lax.rem(y + dy, NY), z, core) for dx, dy in PLANE]
    plane_xy = [(lax.rem(x + dx, NX), lax.rem(y + dy, NY)) for dx, dy in PLANE]
    column = [place(x, y, lax.rem(z + d, NZ), core) for d in range(1, NZ)]
    mirrors = [place(lax.rem(x + d, NX), y, mirror, core) for d in range(NX)]
    holders = [place(lax.rem(x + d, NX), y, z, core) for d in range(1, NX)] + mirrors

    barrier = pltpu.get_barrier_semaphore()
    greeted = [sibling] + plane + column + mirrors[1:]
    for device in greeted:
        pl.semaphore_signal(barrier, inc=1, device_id=device, device_id_type=MESH)

    def remote(src, dst, sems, device):
        return pltpu.make_async_remote_copy(
            src_ref=src, dst_ref=dst, send_sem=sems.at[0], recv_sem=sems.at[1],
            device_id=device, device_id_type=MESH,
        )

    sublane = lax.broadcasted_iota(jnp.int32, (SUB, LANES), 0)
    lane = lax.broadcasted_iota(jnp.int32, (SUB, LANES), 1)
    offset = pair_shift[pair_of_block[wide * 8 + narrow]]
    for g in range(GROUPS):
        energy = core_energy[core_index[g // 2]]
        shift = jnp.zeros((SUB, LANES), F32)
        for j in range(SUB):
            value = frequency[(g % 2) * SUB + j] + energy
            shift = jnp.where(sublane == j, value, shift)
        rows = pl.ds(g * SUB, SUB)
        for b in range(BLOCKS):
            energies = jnp.broadcast_to(virt[b : b + 1, :], (SUB, LANES))
            lev = energies - shift
            inverse = 1.0 / (lev * lev + DAMP * DAMP)
            level[b, rows, :] = lev
            pre_re[b, rows, :] = lev * inverse
            pre_im[b, rows, :] = DAMP * inverse
            den = (shift - offset) - energies
            inverse = 1.0 / (den * den + DAMP * DAMP)
            den_re[b, rows, :] = den * inverse
            den_im[b, rows, :] = DAMP * inverse
    for c in range(2):
        picked[c : c + 1, :] = dipole[pl.ds(core_index[c], 1), :]

    pl.semaphore_wait(barrier, len(greeted))
    for device in holders:
        remote(picked, dip.at[narrow], dip_sems, device).start()
    dip[narrow] = picked[...]

    loads[1].wait()
    high, low = halves(coup[...])
    coup_hi[...] = high
    coup_lo[...] = low
    loads[0].wait()

    others = remote(dip.at[pl.ds(0, BLOCKS - 1)], dip.at[pl.ds(0, BLOCKS - 1)], dip_sems, sibling)
    others.wait_recv()
    for g in range(GROUPS):
        for b in range(BLOCKS):
            source = jnp.broadcast_to(dip[b, g // 2 : g // 2 + 1, :], (SUB, LANES))
            rows = pl.ds(g * SUB, SUB)
            rhs[b, rows, :] = source
            resp[0, b, pl.ds(g * PIECE, SUB), :] = source * pre_re[b, rows, :]
            resp[0, b, pl.ds(g * PIECE + SUB, SUB), :] = source * pre_im[b, rows, :]

    for sweep in range(ITERS):
        for b in range(BLOCKS):
            high, low = halves(resp[sweep, b])
            pieces[:COLS, b * LANES : (b + 1) * LANES] = high
            pieces[COLS:, b * LANES : (b + 1) * LANES] = low
        both = nt(pieces[...], coup_hi[...])
        doubles = both[:COLS] + both[COLS:] + nt(pieces[:COLS, :], coup_lo[...])
        for g in range(GROUPS):
            rows = pl.ds(g * SUB, SUB)
            for b in range(BLOCKS):
                cols = slice(b * LANES, (b + 1) * LANES)
                real = doubles[g * PIECE : g * PIECE + SUB, cols]
                imag = doubles[g * PIECE + SUB : (g + 1) * PIECE, cols]
                q_re, q_im = den_re[b, rows, :], den_im[b, rows, :]
                quotient = jnp.concatenate([real * q_re + imag * q_im, imag * q_re - real * q_im], 0)
                high, low = halves(quotient)
                w_pieces[g * PIECE : (g + 1) * PIECE, cols] = high
                w_pieces[COLS + g * PIECE : COLS + (g + 1) * PIECE, cols] = low
        both = nt(pieces[...], slab[...])
        high, low = halves(both[:COLS] + both[COLS:])
        t_pieces[:COLS, :] = high
        t_pieces[COLS:, :] = low
        if sweep == 0:
            loads[2].wait()

        swap = None
        for turn in range(2):
            side = (1 - core) if turn == 0 else core
            cols = pl.ds(pl.multiple_of(side * (HALF * LANES), HALF * LANES), HALF * LANES)
            both = nn(t_pieces[...], amp[:, cols]) + nn(w_pieces[...], coup_hi[:, cols])
            share = both[:COLS] + both[COLS:] + nn(w_pieces[:COLS, :], coup_lo[:, cols])
            for b in range(HALF):
                part[sweep, side * HALF + b] = share[:, b * LANES : (b + 1) * LANES]
            if turn == 0:
                swap = remote(
                    part.at[sweep, pl.ds(side * HALF, HALF)], from_core.at[sweep],
                    core_sems.at[sweep], sibling,
                )
                swap.start()
        swap.wait_recv()
        for b in range(HALF):
            own[sweep, b] = part[sweep, core * HALF + b] + from_core[sweep, b]

        for i, device in enumerate(plane):
            to_x, to_y = plane_xy[i]
            remote(
                own.at[sweep, to_x, pl.ds(to_y * PIECE, PIECE)], from_plane.at[sweep, i],
                plane_sems.at[sweep], device,
            ).start()
        in_plane = remote(from_plane.at[sweep], from_plane.at[sweep], plane_sems.at[sweep], sibling)
        in_plane.wait_recv()
        total = own[sweep, x, pl.ds(y * PIECE, PIECE), :]
        for i in range(len(plane)):
            total = total + from_plane[sweep, i]
        columns[sweep, z] = total

        for device in column:
            remote(columns.at[sweep, z], columns.at[sweep, z], column_sems.at[sweep], device).start()
        seven = columns.at[sweep, pl.ds(0, NZ - 1)]
        in_column = remote(seven, seven, column_sems.at[sweep], sibling)
        in_column.wait_recv()
        total = columns[sweep, 0]
        for i in range(1, NZ):
            total = total + columns[sweep, i]
        applied[sweep, core * HALF + x, pl.ds(y * PIECE, PIECE), :] = total

        block = applied.at[sweep, core * HALF + x, pl.ds(y * PIECE, PIECE)]
        for device in plane:
            remote(block, block, gather_sems.at[sweep], device).start()
        gathered = remote(from_plane.at[sweep], from_plane.at[sweep], gather_sems.at[sweep], sibling)
        gathered.wait_recv()
        mine = applied.at[sweep, pl.ds(core * HALF, HALF)]
        swap_back = remote(mine, mine, share_sems.at[sweep], sibling)
        swap_back.start()
        swap_back.wait_recv()

        line = jnp.zeros((1, LANES), F32)
        for g in range(GROUPS):
            rows = pl.ds(g * SUB, SUB)
            squares = jnp.zeros((SUB, LANES), F32)
            for b in range(BLOCKS):
                re_rows, im_rows = pl.ds(g * PIECE, SUB), pl.ds(g * PIECE + SUB, SUB)
                re, im = resp[sweep, b, re_rows, :], resp[sweep, b, im_rows, :]
                lev = level[b, rows, :]
                res_re = rhs[b, rows, :] - ((lev * re + DAMP * im) + applied[sweep, b, re_rows, :])
                res_im = -((lev * im - DAMP * re) + applied[sweep, b, im_rows, :])
                squares = squares + (res_re * res_re + res_im * res_im)
                p_re, p_im = pre_re[b, rows, :], pre_im[b, rows, :]
                resp[sweep + 1, b, re_rows, :] = re + (res_re * p_re - res_im * p_im)
                resp[sweep + 1, b, im_rows, :] = im + (res_im * p_re + res_re * p_im)
            summed = jnp.sum(squares, axis=1, keepdims=True)
            spread = jnp.where(lane == sublane + g * SUB, jnp.broadcast_to(summed, (SUB, LANES)), 0.0)
            line = line + jnp.sum(spread, axis=0, keepdims=True)
        rms = jnp.sqrt(line / (2 * BLOCKS * LANES) + 1e-06)
        rms_ref[sweep : sweep + 1, :] = rms[:, : GROUPS * SUB]

    for g in range(GROUPS):
        rows = pl.ds(g * SUB, SUB)
        out_ref[0, rows, :] = resp[ITERS, narrow, pl.ds(g * PIECE, SUB), :]
        out_ref[1, rows, :] = resp[ITERS, narrow, pl.ds(g * PIECE + SUB, SUB), :]

    others.wait_send()
    for sweep in range(ITERS):
        remote(from_core.at[sweep], from_core.at[sweep], core_sems.at[sweep], sibling).wait_send()
        remote(from_core.at[sweep], from_core.at[sweep], share_sems.at[sweep], sibling).wait_send()
        plane_bytes = from_plane.at[sweep]
        remote(plane_bytes, plane_bytes, plane_sems.at[sweep], sibling).wait_send()
        remote(plane_bytes, plane_bytes, gather_sems.at[sweep], sibling).wait_send()
        seven = columns.at[sweep, pl.ds(0, NZ - 1)]
        remote(seven, seven, column_sems.at[sweep], sibling).wait_send()


def per_device(
    amplitudes, integral_slab, coupling, pair_of_block, pair_shift, virt_energy,
    core_energy, core_index, frequency, dipole,
):
    rows, virt_total = amplitudes.shape
    k_total = GROUPS * SUB
    whole = (BLOCKS, k_total, LANES)
    vmem = pl.BlockSpec(memory_space=pltpu.VMEM)
    smem = pl.BlockSpec(memory_space=pltpu.SMEM)
    anywhere = pl.BlockSpec(memory_space=pl.ANY)
    dma = pltpu.SemaphoreType.DMA
    return pl.pallas_call(
        kernel,
        name="response",
        out_shape=(
            jax.ShapeDtypeStruct((2, k_total, LANES), F32),
            jax.ShapeDtypeStruct((ITERS, k_total), F32),
        ),
        in_specs=[smem] * 5 + [vmem] * 2 + [anywhere] * 3,
        out_specs=(vmem, vmem),
        scratch_shapes=[
            pltpu.VMEM((rows, virt_total), BF16),
            pltpu.VMEM((rows, virt_total), BF16),
            pltpu.VMEM((virt_total, virt_total), F32),
            pltpu.VMEM((virt_total, virt_total), BF16),
            pltpu.VMEM((virt_total, virt_total), BF16),
            pltpu.VMEM((2, LANES), F32),
            pltpu.VMEM((BLOCKS, 2, LANES), F32),
            pltpu.VMEM(whole, F32),
            pltpu.VMEM(whole, F32),
            pltpu.VMEM(whole, F32),
            pltpu.VMEM(whole, F32),
            pltpu.VMEM(whole, F32),
            pltpu.VMEM(whole, F32),
            pltpu.VMEM((ITERS + 1, BLOCKS, COLS, LANES), F32),
            pltpu.VMEM((2 * COLS, virt_total), BF16),
            pltpu.VMEM((2 * COLS, rows), BF16),
            pltpu.VMEM((2 * COLS, virt_total), BF16),
            pltpu.VMEM((ITERS, BLOCKS, COLS, LANES), F32),
            pltpu.VMEM((ITERS, HALF, COLS, LANES), F32),
            pltpu.VMEM((ITERS, HALF, COLS, LANES), F32),
            pltpu.VMEM((ITERS, len(PLANE), PIECE, LANES), F32),
            pltpu.VMEM((ITERS, NZ, PIECE, LANES), F32),
            pltpu.VMEM((ITERS, BLOCKS, COLS, LANES), F32),
            pltpu.VMEM((SUB, LANES), F32),
            dma((3,)),
            dma((2,)),
            dma((ITERS, 2)),
            dma((ITERS, 2)),
            dma((ITERS, 2)),
            dma((ITERS, 2)),
            dma((ITERS, 2)),
        ],
        compiler_params=pltpu.CompilerParams(
            collective_id=0, has_side_effects=True, vmem_limit_bytes=56 * 2**20
        ),
    )(
        pair_of_block, pair_shift, core_energy, core_index, frequency,
        virt_energy.reshape(BLOCKS, LANES), dipole, amplitudes, integral_slab, coupling,
    )


def solution(mesh):
    rows = P(("wide", "narrow"), None)
    placed = (rows, rows, P(("wide", "narrow"), None, None)) + (P(),) * 6 + (P(None, "narrow"),)
    return jax.shard_map(
        per_device,
        mesh=mesh,
        in_specs=placed,
        out_specs=(P(None, None, "narrow"), P()),
        check_vma=False,
    )
```

time: 696 us -> 63.4 us (0.09)
  waiting for transfers between devices: 531 us -> 0 us
  blocking collectives: 107 us -> 0 us
  Pallas kernels: 0 us -> 59.9 us
  matrix products: 32.1 us -> 0 us
  between operations: 14.2 us -> 0.64 us
  other arithmetic: 7.74 us -> 0 us
    psum x2 -> x0, waiting for transfers between devices: 531 us -> none  [the longest x1 276 us: per_device(): whole = lax.psum(whole, ('wide', 'narrow'))]
    all_gather x2 -> x0, blocking collectives: 79.5 us -> none  [per_device(): lax.all_gather(response, 'narrow', axis=2, tiled=True)]
    pallas_call x0 -> x1, Pallas kernels: none -> 59.9 us  [per_device(): pl.pallas_call(kernel, name='response', out_shape=(jax.ShapeDtypeStruct((...]
    dot_general x8 -> x0, matrix products: 32.1 us -> none  [the longest x2 12.6 us: absorb(): lax.dot_general(flattened, columns, contract_last, precision=highest, pre...]
    psum x1 -> x0, blocking collectives: 27.1 us -> none  [per_device(): total_squares = lax.psum(partial_squares, 'narrow')]
  transfers between devices with their start and end apart: 2 -> 0, of which waited for: 2 -> 0; matrix products, arithmetic and copies ran while one was open for 0% -> 0% of each run, Pallas kernels for 0% -> 0%
where the time goes in v1:
time: 63.4 us; the launch traced here: 63.2 us
  Pallas kernels  59.9 us (94%)
  local copies, waits for them, and re-layouts  2.6 us (4%)
  between operations  0.64 us (1%)
    pallas_call x1, Pallas kernels, per_device(): pl.pallas_call(kernel, name='response', out_shape=(jax.ShapeDtypeStruct((...  59.9 us
    unnamed x2, local copies, waits for them, and re-layouts  2.6 us

profile of v1, /device:TPU:1, one launch (start us, length us, event | category | flops | bytes accessed | tf_op | source)
XLA Modules:
  0.0 63.2 jit_solution(15476736278545306148)
XLA Ops:
  0.6 59.9 %response.1 = (f32[2,32,128]{2,1,0:T(8,128)}, f32[2,32]{1,0:T(2,128)}) custom-call(s32[256]{0:T(256)} %pair_of_block.1, f32[256]{0:T(256)} %pair_shift.1, f32[64]{0:T(128)} %core_energy.1, s32[2]{0:T(128)} %core_index.1, f32[16]{0:T(128)} %frequency.1, f32[8,128]{1,0:T(8,128)} %bitcast.1, f32[64,128]{1,0:T(8,128)} %dipole.1, bf16[2048,1024]{1,0:T(8,128)(2,1)} %amp_hbm.1, ...), custom_call_target="tpu_custom_call" | custom-call | tf_op jit(solution)/shard_map/response/pallas_call | solution.py:254
  60.6 1.4 %copy.14 = f32[2,32,128]{2,1,0:T(8,128)} copy(f32[2,32,128]{2,1,0:T(8,128)} %get-tuple-element.4) | data formatting | bytes 65536
  62.0 1.2 %copy.15 = f32[2,32]{1,0:T(2,128)} copy(f32[2,32]{1,0:T(2,128)} %get-tuple-element.5) | data formatting | bytes 512

commit v2 on v1

v2 whole, which is shorter than its diff:
```python
from functools import partial

import jax
import jax.numpy as jnp
from jax import lax
from jax.experimental import pallas as pl
from jax.experimental.pallas import tpu as pltpu
from jax.sharding import PartitionSpec as P

DAMP = 0.5
MESH = pl.DeviceIdType.MESH
F32 = jnp.float32
BF16 = jnp.bfloat16

NX, NY, NZ, NZLO = 4, 4, 8, 4
PLANE = tuple((dx, dy) for dx in range(NX) for dy in range(NY))[1:]
GROUPS, SUB, LANES, BLOCKS = 4, 8, 128, 8
PIECE = 2 * SUB
COLS = GROUPS * PIECE
HALF = BLOCKS // 2
HALF_COLS = HALF * LANES
STRIP = 256


def place(x, y, z, core):
    return {
        "wide": (y * NZLO + lax.rem(z, NZLO)) * 2 + core,
        "narrow": x * 2 + z // NZLO,
    }


def nn(left, right):
    return lax.dot_general(left, right, (((1,), (0,)), ((), ())), preferred_element_type=F32)


def halves(value):
    high = value.astype(BF16)
    low = (value - high.astype(F32)).astype(BF16)
    return high, low


def remote(src, dst, sems, device):
    return pltpu.make_async_remote_copy(
        src_ref=src, dst_ref=dst, send_sem=sems.at[0], recv_sem=sems.at[1],
        device_id=device, device_id_type=MESH,
    )


def kernel(
    stop,
    pair_of_block_hbm, pair_shift_hbm, core_energy_hbm, core_index_hbm, frequency_hbm,
    virt_hbm, dipole_hbm, amp_hbm, slab_hbm, coup_hbm,
    out_ref, rms_ref,
    pair_of_block, pair_shift, core_energy, core_index, frequency, virt, dipole,
    amp, slab, coup, slab_t, coup_hi, coup_lo, coup_t_hi, coup_t_lo,
    picked, dip, rhs, pre_re, pre_im, level, den_re, den_im, resp, base, res,
    pieces, t_pieces, w_pieces,
    part, from_core, own, from_plane, columns, applied, final, lines, line_out,
    small_sem, hbm_sem, dip_sems, core_sems, plane_sems, column_sems, gather_sems, share_sem,
    final_sems, line_sems,
):
    wide, narrow = lax.axis_index("wide"), lax.axis_index("narrow")
    x, y, core = narrow // 2, wide // (2 * NZLO), lax.rem(wide, 2)
    z_hi, z_lo = lax.rem(narrow, 2), lax.rem(wide // 2, NZLO)
    z = z_hi * NZLO + z_lo
    mirror = (1 - z_hi) * NZLO + lax.rem(z_lo + 2, NZLO)

    small = [
        pltpu.make_async_copy(src, dst, small_sem.at[i])
        for i, (src, dst) in enumerate((
            (core_index_hbm, core_index), (dipole_hbm, dipole), (virt_hbm, virt),
            (core_energy_hbm, core_energy), (frequency_hbm, frequency),
            (pair_of_block_hbm, pair_of_block), (pair_shift_hbm, pair_shift),
        ))
    ]
    loads = [
        pltpu.make_async_copy(coup_hbm.at[0], coup, hbm_sem.at[0]),
        pltpu.make_async_copy(slab_hbm, slab, hbm_sem.at[1]),
        pltpu.make_async_copy(amp_hbm, amp, hbm_sem.at[2]),
    ]
    for load in small + loads:
        load.start()

    sibling = place(x, y, z, 1 - core)
    plane_xy = [(lax.rem(x + dx, NX), lax.rem(y + dy, NY)) for dx, dy in PLANE]
    plane = [place(to_x, to_y, z, core) for to_x, to_y in plane_xy]
    across = [place(to_x, to_y, z, 1 - core) for to_x, to_y in plane_xy]
    column = [place(x, y, lax.rem(z + d, NZ), core) for d in range(1, NZ)]
    mirrors = [place(lax.rem(x + d, NX), y, mirror, core) for d in range(NX)]
    holders = [place(lax.rem(x + d, NX), y, z, core) for d in range(1, NX)] + mirrors

    barrier = pltpu.get_barrier_semaphore()
    greeted = mirrors[1:] + plane + across + column + [sibling]
    for device in greeted:
        pl.semaphore_signal(barrier, inc=1, device_id=device, device_id_type=MESH)

    for load in small:
        load.wait()
    for c in range(2):
        picked[c : c + 1, :] = dipole[pl.ds(core_index[c], 1), :]
    pl.semaphore_wait(barrier, len(greeted))
    if stop == 0:
        for load in loads:
            load.wait()
        return
    for device in holders:
        remote(picked, dip.at[narrow], dip_sems, device).start()
    dip[narrow] = picked[...]

    sublane = lax.broadcasted_iota(jnp.int32, (SUB, LANES), 0)
    lane = lax.broadcasted_iota(jnp.int32, (SUB, LANES), 1)
    offset = pair_shift[pair_of_block[wide * 8 + narrow]]
    for g in range(GROUPS):
        energy = core_energy[core_index[g // 2]]
        shift = jnp.zeros((SUB, LANES), F32)
        for j in range(SUB):
            value = frequency[(g % 2) * SUB + j] + energy
            shift = jnp.where(sublane == j, value, shift)
        rows = pl.ds(g * SUB, SUB)
        for b in range(BLOCKS):
            energies = jnp.broadcast_to(virt[b : b + 1, :], (SUB, LANES))
            lev = energies - shift
            inverse = 1.0 / (lev * lev + DAMP * DAMP)
            level[b, rows, :] = lev
            pre_re[b, rows, :] = lev * inverse
            pre_im[b, rows, :] = DAMP * inverse
            den = (shift - offset) - energies
            inverse = 1.0 / (den * den + DAMP * DAMP)
            den_re[b, rows, :] = den * inverse
            den_im[b, rows, :] = DAMP * inverse
    if stop == "a":
        for load in loads:
            load.wait()
        dips = dip.at[pl.ds(0, BLOCKS - 1)]
        remote(dips, dips, dip_sems, sibling).wait()
        return

    loads[0].wait()

    def split_rows(i, _):
        rows = pl.ds(pl.multiple_of(i * STRIP, STRIP), STRIP)
        strip = coup[rows, :]
        high, low = halves(strip)
        coup_hi[rows, :] = high
        coup_lo[rows, :] = low
        coup_t_hi[:, rows] = high.T
        coup_t_lo[:, rows] = low.T
        return 0

    lax.fori_loop(0, coup.shape[0] // STRIP, split_rows, 0)
    loads[1].wait()

    def turn_rows(i, _):
        rows = pl.ds(pl.multiple_of(i * STRIP, STRIP), STRIP)
        slab_t[:, rows] = slab[rows, :].T
        return 0

    lax.fori_loop(0, slab.shape[0] // STRIP, turn_rows, 0)
    loads[2].wait()
    if stop == "b":
        dips = dip.at[pl.ds(0, BLOCKS - 1)]
        remote(dips, dips, dip_sems, sibling).wait()
        return

    dips = dip.at[pl.ds(0, BLOCKS - 1)]
    others = remote(dips, dips, dip_sems, sibling)
    others.wait_recv()
    if stop == 1:
        others.wait_send()
        return

    def start_half(half):
        for g in range(GROUPS):
            rows, re_rows, im_rows = pl.ds(g * SUB, SUB), pl.ds(g * PIECE, SUB), pl.ds(g * PIECE + SUB, SUB)
            for j in range(HALF):
                b, cols = half * HALF + j, slice(j * LANES, (j + 1) * LANES)
                source = jnp.broadcast_to(dip[b, g // 2 : g // 2 + 1, :], (SUB, LANES))
                rhs[b, rows, :] = source
                re, im = source * pre_re[b, rows, :], source * pre_im[b, rows, :]
                resp[0, b, re_rows, :] = re
                resp[0, b, im_rows, :] = im
                high, low = halves(jnp.concatenate([re, im], 0))
                pieces[half, g * PIECE : (g + 1) * PIECE, cols] = high
                pieces[half, COLS + g * PIECE : COLS + (g + 1) * PIECE, cols] = low

    def next_half(half):
        for g in range(GROUPS):
            rows, re_rows, im_rows = pl.ds(g * SUB, SUB), pl.ds(g * PIECE, SUB), pl.ds(g * PIECE + SUB, SUB)
            for j in range(HALF):
                b, cols = half * HALF + j, slice(j * LANES, (j + 1) * LANES)
                res_re = base[b, re_rows, :] - applied[b, re_rows, :]
                res_im = base[b, im_rows, :] - applied[b, im_rows, :]
                res[b, re_rows, :] = res_re
                res[b, im_rows, :] = res_im
                p_re, p_im = pre_re[b, rows, :], pre_im[b, rows, :]
                re = resp[0, b, re_rows, :] + (res_re * p_re - res_im * p_im)
                im = resp[0, b, im_rows, :] + (res_im * p_re + res_re * p_im)
                resp[1, b, re_rows, :] = re
                resp[1, b, im_rows, :] = im
                high, low = halves(jnp.concatenate([re, im], 0))
                pieces[half, g * PIECE : (g + 1) * PIECE, cols] = high
                pieces[half, COLS + g * PIECE : COLS + (g + 1) * PIECE, cols] = low

    def expand(half):
        rows = pl.ds(pl.multiple_of(half * HALF_COLS, HALF_COLS), HALF_COLS)
        both = nn(pieces[half], coup_t_hi[rows, :])
        doubles = both[:COLS] + both[COLS:] + nn(pieces[half, :COLS, :], coup_t_lo[rows, :])
        both = nn(pieces[half], slab_t[rows, :])
        return doubles, both[:COLS] + both[COLS:]

    def finish_half(doubles, singles):
        for g in range(GROUPS):
            rows = pl.ds(g * SUB, SUB)
            for b in range(BLOCKS):
                cols = slice(b * LANES, (b + 1) * LANES)
                real = doubles[g * PIECE : g * PIECE + SUB, cols]
                imag = doubles[g * PIECE + SUB : (g + 1) * PIECE, cols]
                q_re, q_im = den_re[b, rows, :], den_im[b, rows, :]
                quotient = jnp.concatenate([real * q_re + imag * q_im, imag * q_re - real * q_im], 0)
                high, low = halves(quotient)
                w_pieces[g * PIECE : (g + 1) * PIECE, cols] = high
                w_pieces[COLS + g * PIECE : COLS + (g + 1) * PIECE, cols] = low
        high, low = halves(singles)
        t_pieces[:COLS, :] = high
        t_pieces[COLS:, :] = low

    def fold(sweep):
        swap = remote(part.at[sweep, 1 - core], from_core.at[sweep], core_sems.at[sweep], sibling)
        for side in (1 - core, core):
            if sweep == 0:
                cols = pl.ds(pl.multiple_of(side * HALF_COLS, HALF_COLS), HALF_COLS)
                from_amp, from_hi, from_lo = amp[:, cols], coup_hi[:, cols], coup_lo[:, cols]
            else:
                spread = [pl.ds(pl.multiple_of((2 * j + side) * LANES, LANES), LANES) for j in range(HALF)]
                from_amp = jnp.concatenate([amp[:, cols] for cols in spread], 1)
                from_hi = jnp.concatenate([coup_hi[:, cols] for cols in spread], 1)
                from_lo = jnp.concatenate([coup_lo[:, cols] for cols in spread], 1)
            both = nn(t_pieces[...], from_amp) + nn(w_pieces[...], from_hi)
            share = both[:COLS] + both[COLS:] + nn(w_pieces[:COLS, :], from_lo)
            if side is core:
                swap.wait_recv()
            for j in range(HALF):
                block = share[:, j * LANES : (j + 1) * LANES]
                if side is core:
                    own[sweep, j] = block + from_core[sweep, j]
                else:
                    part[sweep, side, j] = block
            if side is not core:
                swap.start()
        if stop == 2:
            swap.wait_send()
            return
        for i, device in enumerate(plane):
            to_x, to_y = plane_xy[i]
            remote(
                own.at[sweep, to_x, pl.ds(to_y * PIECE, PIECE)], from_plane.at[sweep, i],
                plane_sems.at[sweep], device,
            ).start()

    def wait_send(ref, sems):
        remote(ref, ref, sems, sibling).wait_send()

    def collect(sweep):
        slots = from_plane.at[sweep]
        remote(slots, slots, plane_sems.at[sweep], sibling).wait_recv()
        total = own[sweep, x, pl.ds(y * PIECE, PIECE), :]
        for i in range(len(plane)):
            total = total + from_plane[sweep, i]
        columns[sweep, z] = total
        if stop == 3:
            wait_send(slots, plane_sems.at[sweep])
            return None
        for device in column:
            remote(columns.at[sweep, z], columns.at[sweep, z], column_sems.at[sweep], device).start()
        seven = columns.at[sweep, pl.ds(0, NZ - 1)]
        remote(seven, seven, column_sems.at[sweep], sibling).wait_recv()
        total = columns[sweep, 0]
        for i in range(1, NZ):
            total = total + columns[sweep, i]
        return total

    def line_of(squares, group):
        summed = jnp.broadcast_to(jnp.sum(squares, axis=1, keepdims=True), (SUB, LANES))
        return jnp.sum(jnp.where(lane == sublane + group * SUB, summed, 0.0), axis=0, keepdims=True)

    def rms_of(line):
        return jnp.sqrt(line / (2 * BLOCKS * LANES) + 1e-06)[:, : GROUPS * SUB]

    start_half(0)
    start_half(1)
    doubles_0, singles_0 = expand(0)
    doubles_1, singles_1 = expand(1)
    finish_half(doubles_0 + doubles_1, singles_0 + singles_1)
    fold(0)
    if stop == 2:
        others.wait_send()
        return
    for g in range(GROUPS):
        rows, re_rows, im_rows = pl.ds(g * SUB, SUB), pl.ds(g * PIECE, SUB), pl.ds(g * PIECE + SUB, SUB)
        for b in range(BLOCKS):
            re, im, lev = resp[0, b, re_rows, :], resp[0, b, im_rows, :], level[b, rows, :]
            base[b, re_rows, :] = rhs[b, rows, :] - (lev * re + DAMP * im)
            base[b, im_rows, :] = -(lev * im - DAMP * re)
    total = collect(0)
    if stop == 3:
        others.wait_send()
        wait_send(from_core.at[0], core_sems.at[0])
        return
    block = applied.at[core * HALF + x, pl.ds(y * PIECE, PIECE)]
    applied[core * HALF + x, pl.ds(y * PIECE, PIECE), :] = total
    if stop == 4:
        others.wait_send()
        wait_send(from_core.at[0], core_sems.at[0])
        wait_send(from_plane.at[0], plane_sems.at[0])
        wait_send(columns.at[0, pl.ds(0, NZ - 1)], column_sems.at[0])
        return
    for device in plane:
        remote(block, block, gather_sems, device).start()
    slots = from_plane.at[0]
    remote(slots, slots, gather_sems, sibling).wait_recv()
    mine = applied.at[pl.ds(core * HALF, HALF)]
    share = remote(mine, mine, share_sem, sibling)
    share.start()
    if stop == 5:
        share.wait()
        others.wait_send()
        wait_send(from_core.at[0], core_sems.at[0])
        wait_send(from_plane.at[0], plane_sems.at[0])
        wait_send(from_plane.at[0], gather_sems)
        wait_send(columns.at[0, pl.ds(0, NZ - 1)], column_sems.at[0])
        return

    next_half(core)
    doubles_0, singles_0 = expand(core)
    share.wait_recv()
    next_half(1 - core)
    doubles_1, singles_1 = expand(1 - core)
    finish_half(doubles_0 + doubles_1, singles_0 + singles_1)
    fold(1)
    line = jnp.zeros((1, LANES), F32)
    for g in range(GROUPS):
        squares = jnp.zeros((SUB, LANES), F32)
        for b in range(BLOCKS):
            res_re, res_im = res[b, pl.ds(g * PIECE, SUB), :], res[b, pl.ds(g * PIECE + SUB, SUB), :]
            squares = squares + (res_re * res_re + res_im * res_im)
        line = line + line_of(squares, g)
    rms_ref[0:1, :] = rms_of(line)
    mine = x * 2 + core
    rows, re_rows = pl.ds(y * SUB, SUB), pl.ds(y * PIECE, SUB)
    im_rows = pl.ds(y * PIECE + SUB, SUB)
    re, im, lev = resp[1, mine, re_rows, :], resp[1, mine, im_rows, :], level[mine, rows, :]
    base_re = rhs[mine, rows, :] - (lev * re + DAMP * im)
    base_im = -(lev * im - DAMP * re)
    total = collect(1)
    if stop != 6:
        res_re, res_im = base_re - total[:SUB], base_im - total[SUB:]
        line = line_of(res_re * res_re + res_im * res_im, y)
        lines[mine * GROUPS + y] = line
        line_out[...] = line
        for device in plane + across + [sibling]:
            remote(line_out, lines.at[mine * GROUPS + y], line_sems, device).start()
        p_re, p_im = pre_re[mine, rows, :], pre_im[mine, rows, :]
        final[core, 0, rows, :] = re + (res_re * p_re - res_im * p_im)
        final[core, 1, rows, :] = im + (res_im * p_re + res_re * p_im)
        block = final.at[core, :, rows]
        near = [place(x, lax.rem(y + d, NY), z, c) for d in range(1, NY) for c in (core, 1 - core)]
        for device in near + [sibling]:
            remote(block, block, final_sems, device).start()
        seven = columns.at[1, pl.ds(0, NZ - 1)]
        remote(seven, seven, final_sems, sibling).wait_recv()
        out_ref[...] = final[z_hi]
        most = lines.at[pl.ds(0, BLOCKS * GROUPS - 1)]
        remote(most, most, line_sems, sibling).wait_recv()
        rms_ref[1:2, :] = rms_of(jnp.sum(lines[...], axis=0))
        wait_send(most, line_sems)
        wait_send(seven, final_sems)

    others.wait_send()
    share.wait_send()
    wait_send(from_plane.at[0], gather_sems)
    for sweep in range(2):
        wait_send(from_core.at[sweep], core_sems.at[sweep])
        wait_send(from_plane.at[sweep], plane_sems.at[sweep])
        wait_send(columns.at[sweep, pl.ds(0, NZ - 1)], column_sems.at[sweep])


def tail(response_in, rms_in, response_out, rms_out):
    response_out[...] = response_in[...]
    rms_out[...] = rms_in[...]


def per_device(
    amplitudes, integral_slab, coupling, pair_of_block, pair_shift, virt_energy,
    core_energy, core_index, frequency, dipole, stop=None, cid=0, name="response",
):
    rows, virt_total = amplitudes.shape
    k_total = GROUPS * SUB
    whole, wide_whole = (BLOCKS, k_total, LANES), (BLOCKS, COLS, LANES)
    vmem = pl.BlockSpec(memory_space=pltpu.VMEM)
    anywhere = pl.BlockSpec(memory_space=pl.ANY)
    dma = pltpu.SemaphoreType.DMA
    shapes = (
        jax.ShapeDtypeStruct((2, k_total, LANES), F32),
        jax.ShapeDtypeStruct((2, k_total), F32),
    )
    response, rms = pl.pallas_call(
        partial(kernel, stop),
        name=name,
        out_shape=shapes,
        in_specs=[anywhere] * 10,
        out_specs=(vmem, vmem),
        scratch_shapes=[
            pltpu.SMEM(pair_of_block.shape, jnp.int32),
            pltpu.SMEM(pair_shift.shape, F32),
            pltpu.SMEM(core_energy.shape, F32),
            pltpu.SMEM(core_index.shape, jnp.int32),
            pltpu.SMEM(frequency.shape, F32),
            pltpu.VMEM((BLOCKS, LANES), F32),
            pltpu.VMEM(dipole.shape, F32),
            pltpu.VMEM((rows, virt_total), BF16),
            pltpu.VMEM((rows, virt_total), BF16),
            pltpu.VMEM((virt_total, virt_total), F32),
            pltpu.VMEM((virt_total, rows), BF16),
            pltpu.VMEM((virt_total, virt_total), BF16),
            pltpu.VMEM((virt_total, virt_total), BF16),
            pltpu.VMEM((virt_total, virt_total), BF16),
            pltpu.VMEM((virt_total, virt_total), BF16),
            pltpu.VMEM((2, LANES), F32),
            pltpu.VMEM((BLOCKS, 2, LANES), F32),
            pltpu.VMEM(whole, F32),
            pltpu.VMEM(whole, F32),
            pltpu.VMEM(whole, F32),
            pltpu.VMEM(whole, F32),
            pltpu.VMEM(whole, F32),
            pltpu.VMEM(whole, F32),
            pltpu.VMEM((2,) + wide_whole, F32),
            pltpu.VMEM(wide_whole, F32),
            pltpu.VMEM(wide_whole, F32),
            pltpu.VMEM((2, 2 * COLS, HALF_COLS), BF16),
            pltpu.VMEM((2 * COLS, rows), BF16),
            pltpu.VMEM((2 * COLS, virt_total), BF16),
            pltpu.VMEM((2, 2, HALF, COLS, LANES), F32),
            pltpu.VMEM((2, HALF, COLS, LANES), F32),
            pltpu.VMEM((2, HALF, COLS, LANES), F32),
            pltpu.VMEM((2, len(PLANE), PIECE, LANES), F32),
            pltpu.VMEM((2, NZ, PIECE, LANES), F32),
            pltpu.VMEM(wide_whole, F32),
            pltpu.VMEM((2, 2, k_total, LANES), F32),
            pltpu.VMEM((BLOCKS * GROUPS, 1, LANES), F32),
            pltpu.VMEM((1, LANES), F32),
            dma((7,)),
            dma((3,)),
            dma((2,)),
            dma((2, 2)),
            dma((2, 2)),
            dma((2, 2)),
            dma((2,)),
            dma((2,)),
            dma((2,)),
            dma((2,)),
        ],
        compiler_params=pltpu.CompilerParams(
            collective_id=cid, has_side_effects=True, vmem_limit_bytes=56 * 2**20
        ),
    )(
        pair_of_block, pair_shift, core_energy, core_index, frequency,
        virt_energy.reshape(BLOCKS, LANES), dipole, amplitudes, integral_slab, coupling,
    )
    return pl.pallas_call(
        tail, name="tail", out_shape=shapes, in_specs=[vmem, vmem], out_specs=(vmem, vmem)
    )(response, rms)


def solution(mesh):
    rows = P(("wide", "narrow"), None)
    placed = (rows, rows, P(("wide", "narrow"), None, None)) + (P(),) * 6 + (P(None, "narrow"),)
    return jax.shard_map(
        per_device,
        mesh=mesh,
        in_specs=placed,
        out_specs=(P(None, None, "narrow"), P()),
        check_vma=False,
    )
```

time: 63.4 us -> 57.1 us (0.901)
  Pallas kernels: 59.9 us -> 56.3 us
  local copies, waits for them, and re-layouts: 2.6 us -> 0 us
    pallas_call x1 -> x2, Pallas kernels: 59.9 us -> 56.3 us  [the longest x1 54.9 us: per_device(): pl.pallas_call(partial(kernel, stop), name=name, out_shape=shapes, in_spe...]
    unnamed x2 -> x0, local copies, waits for them, and re-layouts: 2.6 us -> none
where the time goes in v2:
time: 57.1 us; the launch traced here: 56.9 us
  Pallas kernels  56.3 us (99%)
  between operations  0.64 us (1%)
    pallas_call x1, Pallas kernels, per_device(): pl.pallas_call(partial(kernel, stop), name=name, out_shape=shapes, in_spe...  54.9 us
    pallas_call x1, Pallas kernels, per_device(): pl.pallas_call(tail, name='tail', out_shape=shapes, in_specs=[vmem, vmem]...  1.38 us

profile of v2, /device:TPU:1, one launch (start us, length us, event | category | flops | bytes accessed | tf_op | source)
XLA Modules:
  0.0 56.9 jit_solution(8033174652014373331)
XLA Ops:
  0.6 54.9 %response.1 = (f32[2,32,128]{2,1,0:T(8,128)}, f32[2,32]{1,0:T(2,128)}) custom-call(s32[256]{0:T(256)} %pair_of_block_hbm.1, f32[256]{0:T(256)} %pair_shift_hbm.1, f32[64]{0:T(128)} %core_energy_hbm.1, s32[2]{0:T(128)} %core_index_hbm.1, f32[16]{0:T(128)} %frequency_hbm.1, f32[8,128]{1,0:T(8,128)} %bitcast.1, f32[64,128]{1,0:T(8,128)} %dipole_hbm.1, ...), custom_call_target="tpu_custom_call" | custom-call | tf_op jit(solution)/shard_map/response/pallas_call | solution.py:406
  55.5 1.4 %tail.1 = (f32[2,32,128]{2,1,0:T(8,128)}, f32[2,32]{1,0:T(2,128)}) custom-call(f32[2,32,128]{2,1,0:T(8,128)} %get-tuple-element.4.response_in, f32[2,32]{1,0:T(2,128)} %get-tuple-element.5.rms_in), custom_call_target="tpu_custom_call" | custom-call | tf_op jit(solution)/shard_map/tail/pallas_call | solution.py:469

commit v3 on v2

--- a/solution.py
+++ b/solution.py
@@ -13,7 +13,20 @@
 BF16 = jnp.bfloat16
 
 NX, NY, NZ, NZLO = 4, 4, 8, 4
-PLANE = tuple((dx, dy) for dx in range(NX) for dy in range(NY))[1:]
+
+
+def ring(step, size):
+    return min(step, size - step)
+
+
+PLANE = tuple(
+    sorted(
+        tuple((dx, dy) for dx in range(NX) for dy in range(NY))[1:],
+        key=lambda d: -ring(d[0], NX) - ring(d[1], NY),
+    )
+)
+COLUMN = tuple(sorted(range(1, NZ), key=lambda d: -ring(d, NZ)))
+ALONG = (2, 1, 3, 0)
 GROUPS, SUB, LANES, BLOCKS = 4, 8, 128, 8
 PIECE = 2 * SUB
 COLS = GROUPS * PIECE
@@ -65,6 +78,20 @@
     z = z_hi * NZLO + z_lo
     mirror = (1 - z_hi) * NZLO + lax.rem(z_lo + 2, NZLO)
 
+    sibling = place(x, y, z, 1 - core)
+    plane_xy = [(lax.rem(x + dx, NX), lax.rem(y + dy, NY)) for dx, dy in PLANE]
+    plane = [place(to_x, to_y, z, core) for to_x, to_y in plane_xy]
+    across = [place(to_x, to_y, z, 1 - core) for to_x, to_y in plane_xy]
+    everyone = [device for pair in zip(across, plane) for device in pair] + [sibling]
+    column = [place(x, y, lax.rem(z + d, NZ), core) for d in COLUMN]
+    mirrors = [place(lax.rem(x + d, NX), y, mirror, core) for d in ALONG]
+    holders = mirrors + [place(lax.rem(x + d, NX), y, z, core) for d in ALONG[:-1]]
+
+    barrier = pltpu.get_barrier_semaphore()
+    greeted = mirrors[:-1] + column + everyone
+    for device in greeted:
+        pl.semaphore_signal(barrier, inc=1, device_id=device, device_id_type=MESH)
+
     small = [
         pltpu.make_async_copy(src, dst, small_sem.at[i])
         for i, (src, dst) in enumerate((
@@ -80,19 +107,6 @@
     ]
     for load in small + loads:
         load.start()
-
-    sibling = place(x, y, z, 1 - core)
-    plane_xy = [(lax.rem(x + dx, NX), lax.rem(y + dy, NY)) for dx, dy in PLANE]
-    plane = [place(to_x, to_y, z, core) for to_x, to_y in plane_xy]
-    across = [place(to_x, to_y, z, 1 - core) for to_x, to_y in plane_xy]
-    column = [place(x, y, lax.rem(z + d, NZ), core) for d in range(1, NZ)]
-    mirrors = [place(lax.rem(x + d, NX), y, mirror, core) for d in range(NX)]
-    holders = [place(lax.rem(x + d, NX), y, z, core) for d in range(1, NX)] + mirrors
-
-    barrier = pltpu.get_barrier_semaphore()
-    greeted = mirrors[1:] + plane + across + column + [sibling]
-    for device in greeted:
-        pl.semaphore_signal(barrier, inc=1, device_id=device, device_id_type=MESH)
 
     for load in small:
         load.wait()
@@ -224,41 +238,60 @@
         t_pieces[:COLS, :] = high
         t_pieces[COLS:, :] = low
 
+    parity, far = lax.rem(x, 2), 1 - x // 2
+    strips = (far, 1 - far)
+    reach = ((2 * far + parity, 2 * far + 1 - parity), (3 - 2 * far - parity, 2 - 2 * far + parity))
+
     def fold(sweep):
-        swap = remote(part.at[sweep, 1 - core], from_core.at[sweep], core_sems.at[sweep], sibling)
-        for side in (1 - core, core):
+        def share_of(side, strip):
             if sweep == 0:
-                cols = pl.ds(pl.multiple_of(side * HALF_COLS, HALF_COLS), HALF_COLS)
-                from_amp, from_hi, from_lo = amp[:, cols], coup_hi[:, cols], coup_lo[:, cols]
+                first = pl.multiple_of(side * HALF_COLS + strip * STRIP, STRIP)
+                spans = [pl.ds(first, STRIP)]
             else:
-                spread = [pl.ds(pl.multiple_of((2 * j + side) * LANES, LANES), LANES) for j in range(HALF)]
-                from_amp = jnp.concatenate([amp[:, cols] for cols in spread], 1)
-                from_hi = jnp.concatenate([coup_hi[:, cols] for cols in spread], 1)
-                from_lo = jnp.concatenate([coup_lo[:, cols] for cols in spread], 1)
-            both = nn(t_pieces[...], from_amp) + nn(w_pieces[...], from_hi)
-            share = both[:COLS] + both[COLS:] + nn(w_pieces[:COLS, :], from_lo)
-            if side is core:
-                swap.wait_recv()
-            for j in range(HALF):
-                block = share[:, j * LANES : (j + 1) * LANES]
-                if side is core:
-                    own[sweep, j] = block + from_core[sweep, j]
-                else:
-                    part[sweep, side, j] = block
-            if side is not core:
-                swap.start()
+                spans = [
+                    pl.ds(pl.multiple_of((4 * strip + 2 * i + side) * LANES, LANES), LANES) for i in range(2)
+                ]
+
+            def pick(ref):
+                return jnp.concatenate([ref[:, span] for span in spans], 1) if sweep else ref[:, spans[0]]
+
+            both = nn(t_pieces[...], pick(amp)) + nn(w_pieces[...], pick(coup_hi))
+            return both[:COLS] + both[COLS:] + nn(w_pieces[:COLS, :], pick(coup_lo))
+
+        swaps = []
+        for turn, strip in enumerate(strips):
+            share = share_of(1 - core, strip)
+            for i in range(2):
+                part[sweep, turn, i] = share[:, i * LANES : (i + 1) * LANES]
+            swap = remote(part.at[sweep, turn], from_core.at[sweep, turn], core_sems.at[sweep, turn], sibling)
+            swap.start()
+            swaps.append(swap)
+        slot = 0
+        for turn, strip in enumerate(strips):
+            share = share_of(core, strip)
+            swaps[turn].wait_recv()
+            for i in range(2):
+                own[sweep, 2 * strip + i] = share[:, i * LANES : (i + 1) * LANES] + from_core[sweep, turn, i]
+            if stop == 2:
+                continue
+            for to_x in reach[turn]:
+                for dy in ALONG[: NY if slot < 3 * NY else NY - 1]:
+                    to_y = lax.rem(y + dy, NY)
+                    remote(
+                        own.at[sweep, to_x, pl.ds(to_y * PIECE, PIECE)], from_plane.at[sweep, slot],
+                        plane_sems.at[sweep], place(to_x, to_y, z, core),
+                    ).start()
+                    slot += 1
         if stop == 2:
-            swap.wait_send()
-            return
-        for i, device in enumerate(plane):
-            to_x, to_y = plane_xy[i]
-            remote(
-                own.at[sweep, to_x, pl.ds(to_y * PIECE, PIECE)], from_plane.at[sweep, i],
-                plane_sems.at[sweep], device,
-            ).start()
+            for swap in swaps:
+                swap.wait_send()
 
     def wait_send(ref, sems):
         remote(ref, ref, sems, sibling).wait_send()
+
+    def wait_swaps(sweep):
+        for turn in range(2):
+            wait_send(from_core.at[sweep, turn], core_sems.at[sweep, turn])
 
     def collect(sweep):
         slots = from_plane.at[sweep]
@@ -304,13 +337,13 @@
     total = collect(0)
     if stop == 3:
         others.wait_send()
-        wait_send(from_core.at[0], core_sems.at[0])
+        wait_swaps(0)
         return
     block = applied.at[core * HALF + x, pl.ds(y * PIECE, PIECE)]
     applied[core * HALF + x, pl.ds(y * PIECE, PIECE), :] = total
     if stop == 4:
         others.wait_send()
-        wait_send(from_core.at[0], core_sems.at[0])
+        wait_swaps(0)
         wait_send(from_plane.at[0], plane_sems.at[0])
         wait_send(columns.at[0, pl.ds(0, NZ - 1)], column_sems.at[0])
         return
@@ -324,7 +357,7 @@
     if stop == 5:
         share.wait()
         others.wait_send()
-        wait_send(from_core.at[0], core_sems.at[0])
+        wait_swaps(0)
         wait_send(from_plane.at[0], plane_sems.at[0])
         wait_send(from_plane.at[0], gather_sems)
         wait_send(columns.at[0, pl.ds(0, NZ - 1)], column_sems.at[0])
@@ -357,13 +390,13 @@
         line = line_of(res_re * res_re + res_im * res_im, y)
         lines[mine * GROUPS + y] = line
         line_out[...] = line
-        for device in plane + across + [sibling]:
+        for device in everyone:
             remote(line_out, lines.at[mine * GROUPS + y], line_sems, device).start()
         p_re, p_im = pre_re[mine, rows, :], pre_im[mine, rows, :]
         final[core, 0, rows, :] = re + (res_re * p_re - res_im * p_im)
         final[core, 1, rows, :] = im + (res_im * p_re + res_re * p_im)
         block = final.at[core, :, rows]
-        near = [place(x, lax.rem(y + d, NY), z, c) for d in range(1, NY) for c in (core, 1 - core)]
+        near = [place(x, lax.rem(y + d, NY), z, c) for d in ALONG[:-1] for c in (1 - core, core)]
         for device in near + [sibling]:
             remote(block, block, final_sems, device).start()
         seven = columns.at[1, pl.ds(0, NZ - 1)]
@@ -379,7 +412,7 @@
     share.wait_send()
     wait_send(from_plane.at[0], gather_sems)
     for sweep in range(2):
-        wait_send(from_core.at[sweep], core_sems.at[sweep])
+        wait_swaps(sweep)
         wait_send(from_plane.at[sweep], plane_sems.at[sweep])
         wait_send(columns.at[sweep, pl.ds(0, NZ - 1)], column_sems.at[sweep])
 
@@ -439,8 +472,8 @@
             pltpu.VMEM((2, 2 * COLS, HALF_COLS), BF16),
             pltpu.VMEM((2 * COLS, rows), BF16),
             pltpu.VMEM((2 * COLS, virt_total), BF16),
-            pltpu.VMEM((2, 2, HALF, COLS, LANES), F32),
-            pltpu.VMEM((2, HALF, COLS, LANES), F32),
+            pltpu.VMEM((2, 2, 2, COLS, LANES), F32),
+            pltpu.VMEM((2, 2, 2, COLS, LANES), F32),
             pltpu.VMEM((2, HALF, COLS, LANES), F32),
             pltpu.VMEM((2, len(PLANE), PIECE, LANES), F32),
             pltpu.VMEM((2, NZ, PIECE, LANES), F32),
@@ -451,7 +484,7 @@
             dma((7,)),
             dma((3,)),
             dma((2,)),
-            dma((2, 2)),
+            dma((2, 2, 2)),
             dma((2, 2)),
             dma((2, 2)),
             dma((2,)),

time: 57.1 us -> 54.5 us (0.954)
  Pallas kernels: 56.3 us -> 53.8 us
    pallas_call x1, Pallas kernels: 54.9 us -> 52.4 us  [per_device(): pl.pallas_call(partial(kernel, stop), name=name, out_shape=shapes, in_spe...]
where the time goes in v3:
time: 54.5 us; the launch traced here: 54.4 us
  Pallas kernels  53.8 us (99%)
  between operations  0.64 us (1%)
    pallas_call x1, Pallas kernels, per_device(): pl.pallas_call(partial(kernel, stop), name=name, out_shape=shapes, in_spe...  52.4 us
    pallas_call x1, Pallas kernels, per_device(): pl.pallas_call(tail, name='tail', out_shape=shapes, in_specs=[vmem, vmem]...  1.38 us

profile of v3, /device:TPU:1, one launch (start us, length us, event | category | flops | bytes accessed | tf_op | source)
XLA Modules:
  0.0 54.4 jit_solution(13964310735154369566)
XLA Ops:
  0.6 52.4 %response.1 = (f32[2,32,128]{2,1,0:T(8,128)}, f32[2,32]{1,0:T(2,128)}) custom-call(s32[256]{0:T(256)} %pair_of_block_hbm.1, f32[256]{0:T(256)} %pair_shift_hbm.1, f32[64]{0:T(128)} %core_energy_hbm.1, s32[2]{0:T(128)} %core_index_hbm.1, f32[16]{0:T(128)} %frequency_hbm.1, f32[8,128]{1,0:T(8,128)} %bitcast.1, f32[64,128]{1,0:T(8,128)} %dipole_hbm.1, ...), custom_call_target="tpu_custom_call" | custom-call | tf_op jit(solution)/shard_map/response/pallas_call | solution.py:439
  53.0 1.4 %tail.1 = (f32[2,32,128]{2,1,0:T(8,128)}, f32[2,32]{1,0:T(2,128)}) custom-call(f32[2,32,128]{2,1,0:T(8,128)} %get-tuple-element.4.response_in, f32[2,32]{1,0:T(2,128)} %get-tuple-element.5.rms_in), custom_call_target="tpu_custom_call" | custom-call | tf_op jit(solution)/shard_map/tail/pallas_call | solution.py:502

commit v4 on v3

--- a/solution.py
+++ b/solution.py
@@ -65,9 +65,9 @@
     virt_hbm, dipole_hbm, amp_hbm, slab_hbm, coup_hbm,
     out_ref, rms_ref,
     pair_of_block, pair_shift, core_energy, core_index, frequency, virt, dipole,
-    amp, slab, coup, slab_t, coup_hi, coup_lo, coup_t_hi, coup_t_lo,
+    slab, coup, slab_t, right, coup_t,
     picked, dip, rhs, pre_re, pre_im, level, den_re, den_im, resp, base, res,
-    pieces, t_pieces, w_pieces,
+    pieces, left,
     part, from_core, own, from_plane, columns, applied, final, lines, line_out,
     small_sem, hbm_sem, dip_sems, core_sems, plane_sems, column_sems, gather_sems, share_sem,
     final_sems, line_sems,
@@ -92,6 +92,7 @@
     for device in greeted:
         pl.semaphore_signal(barrier, inc=1, device_id=device, device_id_type=MESH)
 
+    rows_total, virt_total = slab.shape
     small = [
         pltpu.make_async_copy(src, dst, small_sem.at[i])
         for i, (src, dst) in enumerate((
@@ -103,7 +104,7 @@
     loads = [
         pltpu.make_async_copy(coup_hbm.at[0], coup, hbm_sem.at[0]),
         pltpu.make_async_copy(slab_hbm, slab, hbm_sem.at[1]),
-        pltpu.make_async_copy(amp_hbm, amp, hbm_sem.at[2]),
+        pltpu.make_async_copy(amp_hbm, right.at[pl.ds(0, rows_total)], hbm_sem.at[2]),
     ]
     for load in small + loads:
         load.start()
@@ -155,10 +156,14 @@
         rows = pl.ds(pl.multiple_of(i * STRIP, STRIP), STRIP)
         strip = coup[rows, :]
         high, low = halves(strip)
-        coup_hi[rows, :] = high
-        coup_lo[rows, :] = low
-        coup_t_hi[:, rows] = high.T
-        coup_t_lo[:, rows] = low.T
+        start = rows_total + i * STRIP
+        right[pl.ds(pl.multiple_of(start, STRIP), STRIP), :] = high
+        right[pl.ds(pl.multiple_of(start + virt_total, STRIP), STRIP), :] = low
+        high, low = high.T, low.T
+        for half in range(2):
+            own_rows = slice(half * HALF_COLS, (half + 1) * HALF_COLS)
+            coup_t[2 * half * HALF_COLS : (2 * half + 1) * HALF_COLS, rows] = high[own_rows]
+            coup_t[(2 * half + 1) * HALF_COLS : (2 * half + 2) * HALF_COLS, rows] = low[own_rows]
         return 0
 
     lax.fori_loop(0, coup.shape[0] // STRIP, split_rows, 0)
@@ -215,14 +220,17 @@
                 pieces[half, g * PIECE : (g + 1) * PIECE, cols] = high
                 pieces[half, COLS + g * PIECE : COLS + (g + 1) * PIECE, cols] = low
 
+    def joined(both):
+        return both[:COLS] + both[COLS:]
+
     def expand(half):
+        piece = pieces[half]
+        rows = pl.ds(pl.multiple_of(half * 2 * HALF_COLS, HALF_COLS), 2 * HALF_COLS)
+        doubles = nn(jnp.concatenate([piece, piece], 1), coup_t[rows, :])
         rows = pl.ds(pl.multiple_of(half * HALF_COLS, HALF_COLS), HALF_COLS)
-        both = nn(pieces[half], coup_t_hi[rows, :])
-        doubles = both[:COLS] + both[COLS:] + nn(pieces[half, :COLS, :], coup_t_lo[rows, :])
-        both = nn(pieces[half], slab_t[rows, :])
-        return doubles, both[:COLS] + both[COLS:]
-
-    def finish_half(doubles, singles):
+        return joined(doubles), joined(nn(piece, slab_t[rows, :]))
+
+    def finish(doubles, singles):
         for g in range(GROUPS):
             rows = pl.ds(g * SUB, SUB)
             for b in range(BLOCKS):
@@ -232,11 +240,12 @@
                 q_re, q_im = den_re[b, rows, :], den_im[b, rows, :]
                 quotient = jnp.concatenate([real * q_re + imag * q_im, imag * q_re - real * q_im], 0)
                 high, low = halves(quotient)
-                w_pieces[g * PIECE : (g + 1) * PIECE, cols] = high
-                w_pieces[COLS + g * PIECE : COLS + (g + 1) * PIECE, cols] = low
+                cols = slice(rows_total + b * LANES, rows_total + (b + 1) * LANES)
+                left[g * PIECE : (g + 1) * PIECE, cols] = high
+                left[COLS + g * PIECE : COLS + (g + 1) * PIECE, cols] = low
         high, low = halves(singles)
-        t_pieces[:COLS, :] = high
-        t_pieces[COLS:, :] = low
+        left[:COLS, :rows_total] = high
+        left[COLS:, :rows_total] = low
 
     parity, far = lax.rem(x, 2), 1 - x // 2
     strips = (far, 1 - far)
@@ -252,11 +261,9 @@
                     pl.ds(pl.multiple_of((4 * strip + 2 * i + side) * LANES, LANES), LANES) for i in range(2)
                 ]
 
-            def pick(ref):
-                return jnp.concatenate([ref[:, span] for span in spans], 1) if sweep else ref[:, spans[0]]
-
-            both = nn(t_pieces[...], pick(amp)) + nn(w_pieces[...], pick(coup_hi))
-            return both[:COLS] + both[COLS:] + nn(w_pieces[:COLS, :], pick(coup_lo))
+            strip_of = [right[:, span] for span in spans]
+            strip_of = jnp.concatenate(strip_of, 1) if sweep else strip_of[0]
+            return joined(nn(jnp.concatenate([left[...], left[:, rows_total:]], 1), strip_of))
 
         swaps = []
         for turn, strip in enumerate(strips):
@@ -321,9 +328,9 @@
 
     start_half(0)
     start_half(1)
-    doubles_0, singles_0 = expand(0)
-    doubles_1, singles_1 = expand(1)
-    finish_half(doubles_0 + doubles_1, singles_0 + singles_1)
+    both = [pieces[0], pieces[1]]
+    doubles = joined(nn(jnp.concatenate([both[0], both[0], both[1], both[1]], 1), coup_t[...]))
+    finish(doubles, joined(nn(jnp.concatenate(both, 1), slab_t[...])))
     fold(0)
     if stop == 2:
         others.wait_send()
@@ -368,7 +375,7 @@
     share.wait_recv()
     next_half(1 - core)
     doubles_1, singles_1 = expand(1 - core)
-    finish_half(doubles_0 + doubles_1, singles_0 + singles_1)
+    finish(doubles_0 + doubles_1, singles_0 + singles_1)
     fold(1)
     line = jnp.zeros((1, LANES), F32)
     for g in range(GROUPS):
@@ -439,7 +446,7 @@
     response, rms = pl.pallas_call(
         partial(kernel, stop),
         name=name,
-        out_shape=shapes,
+        out_shape=tuple(pltpu.VMEM(shape.shape, shape.dtype) for shape in shapes),
         in_specs=[anywhere] * 10,
         out_specs=(vmem, vmem),
         scratch_shapes=[
@@ -451,13 +458,10 @@
             pltpu.VMEM((BLOCKS, LANES), F32),
             pltpu.VMEM(dipole.shape, F32),
             pltpu.VMEM((rows, virt_total), BF16),
-            pltpu.VMEM((rows, virt_total), BF16),
             pltpu.VMEM((virt_total, virt_total), F32),
             pltpu.VMEM((virt_total, rows), BF16),
-            pltpu.VMEM((virt_total, virt_total), BF16),
-            pltpu.VMEM((virt_total, virt_total), BF16),
-            pltpu.VMEM((virt_total, virt_total), BF16),
-            pltpu.VMEM((virt_total, virt_total), BF16),
+            pltpu.VMEM((rows + 2 * virt_total, virt_total), BF16),
+            pltpu.VMEM((2 * virt_total, virt_total), BF16),
             pltpu.VMEM((2, LANES), F32),
             pltpu.VMEM((BLOCKS, 2, LANES), F32),
             pltpu.VMEM(whole, F32),
@@ -470,8 +474,7 @@
             pltpu.VMEM(wide_whole, F32),
             pltpu.VMEM(wide_whole, F32),
             pltpu.VMEM((2, 2 * COLS, HALF_COLS), BF16),
-            pltpu.VMEM((2 * COLS, rows), BF16),
-            pltpu.VMEM((2 * COLS, virt_total), BF16),
+            pltpu.VMEM((2 * COLS, rows + virt_total), BF16),
             pltpu.VMEM((2, 2, 2, COLS, LANES), F32),
             pltpu.VMEM((2, 2, 2, COLS, LANES), F32),
             pltpu.VMEM((2, HALF, COLS, LANES), F32),
@@ -501,7 +504,7 @@
     )
     return pl.pallas_call(
         tail, name="tail", out_shape=shapes, in_specs=[vmem, vmem], out_specs=(vmem, vmem)
-    )(response, rms)
+    )(*(pltpu.with_memory_space_constraint(value, pltpu.VMEM) for value in (response, rms)))
 
 
 def solution(mesh):

time: 54.5 us -> 53 us (0.972)
  Pallas kernels: 53.8 us -> 52.3 us
    pallas_call x1, Pallas kernels: 1.38 us -> 0.62 us  [per_device(): pl.pallas_call(tail, name='tail', out_shape=shapes, in_specs=[vmem, vmem]...]
    pallas_call x1, Pallas kernels: 52.4 us -> 51.7 us  [per_device(): pl.pallas_call(partial(kernel, stop), name=name, out_shape=tuple((pltpu.V...]
where the time goes in v4:
time: 53 us; the launch traced here: 52.9 us
  Pallas kernels  52.3 us (99%)
  between operations  0.64 us (1%)
    pallas_call x1, Pallas kernels, per_device(): pl.pallas_call(partial(kernel, stop), name=name, out_shape=tuple((pltpu.V...  51.7 us

profile of v4, /device:TPU:1, one launch (start us, length us, event | category | flops | bytes accessed | tf_op | source)
XLA Modules:
  0.0 52.9 jit_solution(412952883603292351)
XLA Ops:
  0.6 51.7 %response.1 = (f32[2,32,128]{2,1,0:T(8,128)S(1)}, f32[2,32]{1,0:T(2,128)S(1)}) custom-call(s32[256]{0:T(256)} %pair_of_block_hbm.1, f32[256]{0:T(256)} %pair_shift_hbm.1, f32[64]{0:T(128)} %core_energy_hbm.1, s32[2]{0:T(128)} %core_index_hbm.1, f32[16]{0:T(128)} %frequency_hbm.1, f32[8,128]{1,0:T(8,128)} %bitcast.1, f32[64,128]{1,0:T(8,128)} %dipole_hbm.1, ...), custom_call_target="tpu_custom_call" | custom-call | tf_op jit(solution)/shard_map/response/pallas_call | solution.py:446
  52.3 0.6 %tail.1 = (f32[2,32,128]{2,1,0:T(8,128)}, f32[2,32]{1,0:T(2,128)}) custom-call(f32[2,32,128]{2,1,0:T(8,128)S(1)} %get-tuple-element.4.response_in, f32[2,32]{1,0:T(2,128)S(1)} %get-tuple-element.5.rms_in), custom_call_target="tpu_custom_call" | custom-call | tf_op jit(solution)/shard_map/tail/pallas_call | solution.py:505

commit v5 on v4

--- a/solution.py
+++ b/solution.py
@@ -1,5 +1,3 @@
-from functools import partial
-
 import jax
 import jax.numpy as jnp
 from jax import lax
@@ -42,6 +40,10 @@
     }
 
 
+def spot(block):
+    return (block % 2) * HALF + block // 2
+
+
 def nn(left, right):
     return lax.dot_general(left, right, (((1,), (0,)), ((), ())), preferred_element_type=F32)
 
@@ -60,7 +62,6 @@
 
 
 def kernel(
-    stop,
     pair_of_block_hbm, pair_shift_hbm, core_energy_hbm, core_index_hbm, frequency_hbm,
     virt_hbm, dipole_hbm, amp_hbm, slab_hbm, coup_hbm,
     out_ref, rms_ref,
@@ -85,10 +86,12 @@
     everyone = [device for pair in zip(across, plane) for device in pair] + [sibling]
     column = [place(x, y, lax.rem(z + d, NZ), core) for d in COLUMN]
     mirrors = [place(lax.rem(x + d, NX), y, mirror, core) for d in ALONG]
-    holders = mirrors + [place(lax.rem(x + d, NX), y, z, core) for d in ALONG[:-1]]
+    beside = [place(lax.rem(x + d, NX), y, z, core) for d in ALONG[:-1]]
 
     barrier = pltpu.get_barrier_semaphore()
-    greeted = mirrors[:-1] + column + everyone
+    far_plane = sum(ring(dx, NX) + ring(dy, NY) > 2 for dx, dy in PLANE)
+    greeted = mirrors[:1] + column[:1] + everyone[: 2 * far_plane] + mirrors[1:-1] + column[1:]
+    greeted = greeted + everyone[2 * far_plane :]
     for device in greeted:
         pl.semaphore_signal(barrier, inc=1, device_id=device, device_id_type=MESH)
 
@@ -104,7 +107,13 @@
     loads = [
         pltpu.make_async_copy(coup_hbm.at[0], coup, hbm_sem.at[0]),
         pltpu.make_async_copy(slab_hbm, slab, hbm_sem.at[1]),
-        pltpu.make_async_copy(amp_hbm, right.at[pl.ds(0, rows_total)], hbm_sem.at[2]),
+    ] + [
+        pltpu.make_async_copy(
+            amp_hbm.at[:, pl.ds(b * LANES, LANES)],
+            right.at[pl.ds(0, rows_total), pl.ds(spot(b) * LANES, LANES)],
+            hbm_sem.at[2 + b],
+        )
+        for b in range(BLOCKS)
     ]
     for load in small + loads:
         load.start()
@@ -114,12 +123,10 @@
     for c in range(2):
         picked[c : c + 1, :] = dipole[pl.ds(core_index[c], 1), :]
     pl.semaphore_wait(barrier, len(greeted))
-    if stop == 0:
-        for load in loads:
-            load.wait()
-        return
-    for device in holders:
-        remote(picked, dip.at[narrow], dip_sems, device).start()
+    for device in mirrors:
+        remote(picked, dip.at[narrow], dip_sems.at[1], device).start()
+    for device in beside:
+        remote(picked, dip.at[narrow], dip_sems.at[0], device).start()
     dip[narrow] = picked[...]
 
     sublane = lax.broadcasted_iota(jnp.int32, (SUB, LANES), 0)
@@ -136,20 +143,13 @@
             energies = jnp.broadcast_to(virt[b : b + 1, :], (SUB, LANES))
             lev = energies - shift
             inverse = 1.0 / (lev * lev + DAMP * DAMP)
-            level[b, rows, :] = lev
-            pre_re[b, rows, :] = lev * inverse
-            pre_im[b, rows, :] = DAMP * inverse
+            level[spot(b), rows, :] = lev
+            pre_re[spot(b), rows, :] = lev * inverse
+            pre_im[spot(b), rows, :] = DAMP * inverse
             den = (shift - offset) - energies
             inverse = 1.0 / (den * den + DAMP * DAMP)
             den_re[b, rows, :] = den * inverse
             den_im[b, rows, :] = DAMP * inverse
-    if stop == "a":
-        for load in loads:
-            load.wait()
-        dips = dip.at[pl.ds(0, BLOCKS - 1)]
-        remote(dips, dips, dip_sems, sibling).wait()
-        return
-
     loads[0].wait()
 
     def split_rows(i, _):
@@ -157,13 +157,15 @@
         strip = coup[rows, :]
         high, low = halves(strip)
         start = rows_total + i * STRIP
-        right[pl.ds(pl.multiple_of(start, STRIP), STRIP), :] = high
-        right[pl.ds(pl.multiple_of(start + virt_total, STRIP), STRIP), :] = low
+        for b in range(BLOCKS):
+            cols, there = slice(b * LANES, (b + 1) * LANES), slice(spot(b) * LANES, (spot(b) + 1) * LANES)
+            right[pl.ds(pl.multiple_of(start, STRIP), STRIP), there] = high[:, cols]
+            right[pl.ds(pl.multiple_of(start + virt_total, STRIP), STRIP), there] = low[:, cols]
         high, low = high.T, low.T
-        for half in range(2):
-            own_rows = slice(half * HALF_COLS, (half + 1) * HALF_COLS)
-            coup_t[2 * half * HALF_COLS : (2 * half + 1) * HALF_COLS, rows] = high[own_rows]
-            coup_t[(2 * half + 1) * HALF_COLS : (2 * half + 2) * HALF_COLS, rows] = low[own_rows]
+        for b in range(BLOCKS):
+            cols, there = slice(b * LANES, (b + 1) * LANES), (b % 2) * 2 * HALF_COLS + (b // 2) * LANES
+            coup_t[there : there + LANES, rows] = high[cols]
+            coup_t[there + HALF_COLS : there + HALF_COLS + LANES, rows] = low[cols]
         return 0
 
     lax.fori_loop(0, coup.shape[0] // STRIP, split_rows, 0)
@@ -171,29 +173,23 @@
 
     def turn_rows(i, _):
         rows = pl.ds(pl.multiple_of(i * STRIP, STRIP), STRIP)
-        slab_t[:, rows] = slab[rows, :].T
+        turned = slab[rows, :].T
+        for b in range(BLOCKS):
+            slab_t[spot(b) * LANES : (spot(b) + 1) * LANES, rows] = turned[b * LANES : (b + 1) * LANES]
         return 0
 
     lax.fori_loop(0, slab.shape[0] // STRIP, turn_rows, 0)
-    loads[2].wait()
-    if stop == "b":
-        dips = dip.at[pl.ds(0, BLOCKS - 1)]
-        remote(dips, dips, dip_sems, sibling).wait()
-        return
-
-    dips = dip.at[pl.ds(0, BLOCKS - 1)]
-    others = remote(dips, dips, dip_sems, sibling)
-    others.wait_recv()
-    if stop == 1:
-        others.wait_send()
-        return
+    for load in loads[2:]:
+        load.wait()
+    same = remote(dip.at[pl.ds(0, NX - 1)], dip.at[pl.ds(0, NX - 1)], dip_sems.at[0], sibling)
+    mirrored = remote(dip.at[pl.ds(0, NX)], dip.at[pl.ds(0, NX)], dip_sems.at[1], sibling)
 
     def start_half(half):
         for g in range(GROUPS):
             rows, re_rows, im_rows = pl.ds(g * SUB, SUB), pl.ds(g * PIECE, SUB), pl.ds(g * PIECE + SUB, SUB)
             for j in range(HALF):
                 b, cols = half * HALF + j, slice(j * LANES, (j + 1) * LANES)
-                source = jnp.broadcast_to(dip[b, g // 2 : g // 2 + 1, :], (SUB, LANES))
+                source = jnp.broadcast_to(dip[2 * j + half, g // 2 : g // 2 + 1, :], (SUB, LANES))
                 rhs[b, rows, :] = source
                 re, im = source * pre_re[b, rows, :], source * pre_im[b, rows, :]
                 resp[0, b, re_rows, :] = re
@@ -253,17 +249,8 @@
 
     def fold(sweep):
         def share_of(side, strip):
-            if sweep == 0:
-                first = pl.multiple_of(side * HALF_COLS + strip * STRIP, STRIP)
-                spans = [pl.ds(first, STRIP)]
-            else:
-                spans = [
-                    pl.ds(pl.multiple_of((4 * strip + 2 * i + side) * LANES, LANES), LANES) for i in range(2)
-                ]
-
-            strip_of = [right[:, span] for span in spans]
-            strip_of = jnp.concatenate(strip_of, 1) if sweep else strip_of[0]
-            return joined(nn(jnp.concatenate([left[...], left[:, rows_total:]], 1), strip_of))
+            cols = pl.ds(pl.multiple_of(side * HALF_COLS + strip * STRIP, STRIP), STRIP)
+            return joined(nn(jnp.concatenate([left[...], left[:, rows_total:]], 1), right[:, cols]))
 
         swaps = []
         for turn, strip in enumerate(strips):
@@ -279,8 +266,6 @@
             swaps[turn].wait_recv()
             for i in range(2):
                 own[sweep, 2 * strip + i] = share[:, i * LANES : (i + 1) * LANES] + from_core[sweep, turn, i]
-            if stop == 2:
-                continue
             for to_x in reach[turn]:
                 for dy in ALONG[: NY if slot < 3 * NY else NY - 1]:
                     to_y = lax.rem(y + dy, NY)
@@ -289,12 +274,12 @@
                         plane_sems.at[sweep], place(to_x, to_y, z, core),
                     ).start()
                     slot += 1
-        if stop == 2:
-            for swap in swaps:
-                swap.wait_send()
-
     def wait_send(ref, sems):
         remote(ref, ref, sems, sibling).wait_send()
+
+    def wait_dipoles():
+        same.wait_send()
+        mirrored.wait_send()
 
     def wait_swaps(sweep):
         for turn in range(2):
@@ -307,9 +292,6 @@
         for i in range(len(plane)):
             total = total + from_plane[sweep, i]
         columns[sweep, z] = total
-        if stop == 3:
-            wait_send(slots, plane_sems.at[sweep])
-            return None
         for device in column:
             remote(columns.at[sweep, z], columns.at[sweep, z], column_sems.at[sweep], device).start()
         seven = columns.at[sweep, pl.ds(0, NZ - 1)]
@@ -326,15 +308,14 @@
     def rms_of(line):
         return jnp.sqrt(line / (2 * BLOCKS * LANES) + 1e-06)[:, : GROUPS * SUB]
 
-    start_half(0)
-    start_half(1)
-    both = [pieces[0], pieces[1]]
-    doubles = joined(nn(jnp.concatenate([both[0], both[0], both[1], both[1]], 1), coup_t[...]))
-    finish(doubles, joined(nn(jnp.concatenate(both, 1), slab_t[...])))
+    same.wait_recv()
+    start_half(z_hi)
+    doubles_0, singles_0 = expand(z_hi)
+    mirrored.wait_recv()
+    start_half(1 - z_hi)
+    doubles_1, singles_1 = expand(1 - z_hi)
+    finish(doubles_0 + doubles_1, singles_0 + singles_1)
     fold(0)
-    if stop == 2:
-        others.wait_send()
-        return
     for g in range(GROUPS):
         rows, re_rows, im_rows = pl.ds(g * SUB, SUB), pl.ds(g * PIECE, SUB), pl.ds(g * PIECE + SUB, SUB)
         for b in range(BLOCKS):
@@ -342,18 +323,8 @@
             base[b, re_rows, :] = rhs[b, rows, :] - (lev * re + DAMP * im)
             base[b, im_rows, :] = -(lev * im - DAMP * re)
     total = collect(0)
-    if stop == 3:
-        others.wait_send()
-        wait_swaps(0)
-        return
     block = applied.at[core * HALF + x, pl.ds(y * PIECE, PIECE)]
     applied[core * HALF + x, pl.ds(y * PIECE, PIECE), :] = total
-    if stop == 4:
-        others.wait_send()
-        wait_swaps(0)
-        wait_send(from_plane.at[0], plane_sems.at[0])
-        wait_send(columns.at[0, pl.ds(0, NZ - 1)], column_sems.at[0])
-        return
     for device in plane:
         remote(block, block, gather_sems, device).start()
     slots = from_plane.at[0]
@@ -361,15 +332,6 @@
     mine = applied.at[pl.ds(core * HALF, HALF)]
     share = remote(mine, mine, share_sem, sibling)
     share.start()
-    if stop == 5:
-        share.wait()
-        others.wait_send()
-        wait_swaps(0)
-        wait_send(from_plane.at[0], plane_sems.at[0])
-        wait_send(from_plane.at[0], gather_sems)
-        wait_send(columns.at[0, pl.ds(0, NZ - 1)], column_sems.at[0])
-        return
-
     next_half(core)
     doubles_0, singles_0 = expand(core)
     share.wait_recv()
@@ -385,37 +347,36 @@
             squares = squares + (res_re * res_re + res_im * res_im)
         line = line + line_of(squares, g)
     rms_ref[0:1, :] = rms_of(line)
-    mine = x * 2 + core
+    mine = core * HALF + x
     rows, re_rows = pl.ds(y * SUB, SUB), pl.ds(y * PIECE, SUB)
     im_rows = pl.ds(y * PIECE + SUB, SUB)
     re, im, lev = resp[1, mine, re_rows, :], resp[1, mine, im_rows, :], level[mine, rows, :]
     base_re = rhs[mine, rows, :] - (lev * re + DAMP * im)
     base_im = -(lev * im - DAMP * re)
     total = collect(1)
-    if stop != 6:
-        res_re, res_im = base_re - total[:SUB], base_im - total[SUB:]
-        line = line_of(res_re * res_re + res_im * res_im, y)
-        lines[mine * GROUPS + y] = line
-        line_out[...] = line
-        for device in everyone:
-            remote(line_out, lines.at[mine * GROUPS + y], line_sems, device).start()
-        p_re, p_im = pre_re[mine, rows, :], pre_im[mine, rows, :]
-        final[core, 0, rows, :] = re + (res_re * p_re - res_im * p_im)
-        final[core, 1, rows, :] = im + (res_im * p_re + res_re * p_im)
-        block = final.at[core, :, rows]
-        near = [place(x, lax.rem(y + d, NY), z, c) for d in ALONG[:-1] for c in (1 - core, core)]
-        for device in near + [sibling]:
-            remote(block, block, final_sems, device).start()
-        seven = columns.at[1, pl.ds(0, NZ - 1)]
-        remote(seven, seven, final_sems, sibling).wait_recv()
-        out_ref[...] = final[z_hi]
-        most = lines.at[pl.ds(0, BLOCKS * GROUPS - 1)]
-        remote(most, most, line_sems, sibling).wait_recv()
-        rms_ref[1:2, :] = rms_of(jnp.sum(lines[...], axis=0))
-        wait_send(most, line_sems)
-        wait_send(seven, final_sems)
-
-    others.wait_send()
+    res_re, res_im = base_re - total[:SUB], base_im - total[SUB:]
+    line = line_of(res_re * res_re + res_im * res_im, y)
+    lines[mine * GROUPS + y] = line
+    line_out[...] = line
+    for device in everyone:
+        remote(line_out, lines.at[mine * GROUPS + y], line_sems, device).start()
+    p_re, p_im = pre_re[mine, rows, :], pre_im[mine, rows, :]
+    final[core, 0, rows, :] = re + (res_re * p_re - res_im * p_im)
+    final[core, 1, rows, :] = im + (res_im * p_re + res_re * p_im)
+    block = final.at[core, :, rows]
+    near = [place(x, lax.rem(y + d, NY), z, c) for d in ALONG[:-1] for c in (1 - core, core)]
+    for device in near + [sibling]:
+        remote(block, block, final_sems, device).start()
+    seven = columns.at[1, pl.ds(0, NZ - 1)]
+    remote(seven, seven, final_sems, sibling).wait_recv()
+    out_ref[...] = final[z_hi]
+    most = lines.at[pl.ds(0, BLOCKS * GROUPS - 1)]
+    remote(most, most, line_sems, sibling).wait_recv()
+    rms_ref[1:2, :] = rms_of(jnp.sum(lines[...], axis=0))
+    wait_send(most, line_sems)
+    wait_send(seven, final_sems)
+
+    wait_dipoles()
     share.wait_send()
     wait_send(from_plane.at[0], gather_sems)
     for sweep in range(2):
@@ -431,7 +392,7 @@
 
 def per_device(
     amplitudes, integral_slab, coupling, pair_of_block, pair_shift, virt_energy,
-    core_energy, core_index, frequency, dipole, stop=None, cid=0, name="response",
+    core_energy, core_index, frequency, dipole,
 ):
     rows, virt_total = amplitudes.shape
     k_total = GROUPS * SUB
@@ -444,8 +405,8 @@
         jax.ShapeDtypeStruct((2, k_total), F32),
     )
     response, rms = pl.pallas_call(
-        partial(kernel, stop),
-        name=name,
+        kernel,
+        name="response",
         out_shape=tuple(pltpu.VMEM(shape.shape, shape.dtype) for shape in shapes),
         in_specs=[anywhere] * 10,
         out_specs=(vmem, vmem),
@@ -485,8 +446,8 @@
             pltpu.VMEM((BLOCKS * GROUPS, 1, LANES), F32),
             pltpu.VMEM((1, LANES), F32),
             dma((7,)),
-            dma((3,)),
-            dma((2,)),
+            dma((2 + BLOCKS,)),
+            dma((2, 2)),
             dma((2, 2, 2)),
             dma((2, 2)),
             dma((2, 2)),
@@ -496,7 +457,7 @@
             dma((2,)),
         ],
         compiler_params=pltpu.CompilerParams(
-            collective_id=cid, has_side_effects=True, vmem_limit_bytes=56 * 2**20
+            collective_id=0, has_side_effects=True, vmem_limit_bytes=56 * 2**20
         ),
     )(
         pair_of_block, pair_shift, core_energy, core_index, frequency,

time: 53 us -> 53.1 us (level)
  no operation moved by 1% of the time
where the time goes in v5:
time: 53.1 us; the launch traced here: 53 us
  Pallas kernels  52.3 us (98%)
  between operations  0.64 us (1%)
    pallas_call x1, Pallas kernels, per_device(): pl.pallas_call(kernel, name='response', out_shape=tuple((pltpu.VMEM(shape...  51.7 us

profile of v5, /device:TPU:1, one launch (start us, length us, event | category | flops | bytes accessed | tf_op | source)
XLA Modules:
  0.0 53.0 jit_solution(8825093322228063605)
XLA Ops:
  0.6 51.7 %response.1 = (f32[2,32,128]{2,1,0:T(8,128)S(1)}, f32[2,32]{1,0:T(2,128)S(1)}) custom-call(s32[256]{0:T(256)} %pair_of_block_hbm.1, f32[256]{0:T(256)} %pair_shift_hbm.1, f32[64]{0:T(128)} %core_energy_hbm.1, s32[2]{0:T(128)} %core_index_hbm.1, f32[16]{0:T(128)} %frequency_hbm.1, f32[8,128]{1,0:T(8,128)} %bitcast.1, f32[64,128]{1,0:T(8,128)} %dipole_hbm.1, ...), custom_call_target="tpu_custom_call" | custom-call | tf_op jit(solution)/shard_map/response/pallas_call | solution.py:407
  52.4 0.6 %tail.1 = (f32[2,32,128]{2,1,0:T(8,128)}, f32[2,32]{1,0:T(2,128)}) custom-call(f32[2,32,128]{2,1,0:T(8,128)S(1)} %get-tuple-element.4.response_in, f32[2,32]{1,0:T(2,128)S(1)} %get-tuple-element.5.rms_in), custom_call_target="tpu_custom_call" | custom-call | tf_op jit(solution)/shard_map/tail/pallas_call | solution.py:466

commit v6 on v5

--- a/solution.py
+++ b/solution.py
@@ -77,8 +77,14 @@
     x, y, core = narrow // 2, wide // (2 * NZLO), lax.rem(wide, 2)
     z_hi, z_lo = lax.rem(narrow, 2), lax.rem(wide // 2, NZLO)
     z = z_hi * NZLO + z_lo
+    rows_total, virt_total = slab.shape
     mirror = (1 - z_hi) * NZLO + lax.rem(z_lo + 2, NZLO)
 
+    loads = [
+        pltpu.make_async_copy(coup_hbm.at[0], coup, hbm_sem.at[0]),
+        pltpu.make_async_copy(slab_hbm, slab, hbm_sem.at[1]),
+        pltpu.make_async_copy(amp_hbm, right.at[pl.ds(0, rows_total)], hbm_sem.at[2]),
+    ]
     sibling = place(x, y, z, 1 - core)
     plane_xy = [(lax.rem(x + dx, NX), lax.rem(y + dy, NY)) for dx, dy in PLANE]
     plane = [place(to_x, to_y, z, core) for to_x, to_y in plane_xy]
@@ -89,13 +95,10 @@
     beside = [place(lax.rem(x + d, NX), y, z, core) for d in ALONG[:-1]]
 
     barrier = pltpu.get_barrier_semaphore()
-    far_plane = sum(ring(dx, NX) + ring(dy, NY) > 2 for dx, dy in PLANE)
-    greeted = mirrors[:1] + column[:1] + everyone[: 2 * far_plane] + mirrors[1:-1] + column[1:]
-    greeted = greeted + everyone[2 * far_plane :]
+    greeted = mirrors[:-1] + column
     for device in greeted:
         pl.semaphore_signal(barrier, inc=1, device_id=device, device_id_type=MESH)
 
-    rows_total, virt_total = slab.shape
     small = [
         pltpu.make_async_copy(src, dst, small_sem.at[i])
         for i, (src, dst) in enumerate((
@@ -104,30 +107,15 @@
             (pair_of_block_hbm, pair_of_block), (pair_shift_hbm, pair_shift),
         ))
     ]
-    loads = [
-        pltpu.make_async_copy(coup_hbm.at[0], coup, hbm_sem.at[0]),
-        pltpu.make_async_copy(slab_hbm, slab, hbm_sem.at[1]),
-    ] + [
-        pltpu.make_async_copy(
-            amp_hbm.at[:, pl.ds(b * LANES, LANES)],
-            right.at[pl.ds(0, rows_total), pl.ds(spot(b) * LANES, LANES)],
-            hbm_sem.at[2 + b],
-        )
-        for b in range(BLOCKS)
-    ]
-    for load in small + loads:
+    for load in small + loads[:2]:
         load.start()
+    for device in everyone:
+        pl.semaphore_signal(barrier, inc=1, device_id=device, device_id_type=MESH)
 
     for load in small:
         load.wait()
     for c in range(2):
         picked[c : c + 1, :] = dipole[pl.ds(core_index[c], 1), :]
-    pl.semaphore_wait(barrier, len(greeted))
-    for device in mirrors:
-        remote(picked, dip.at[narrow], dip_sems.at[1], device).start()
-    for device in beside:
-        remote(picked, dip.at[narrow], dip_sems.at[0], device).start()
-    dip[narrow] = picked[...]
 
     sublane = lax.broadcasted_iota(jnp.int32, (SUB, LANES), 0)
     lane = lax.broadcasted_iota(jnp.int32, (SUB, LANES), 1)
@@ -150,6 +138,15 @@
             inverse = 1.0 / (den * den + DAMP * DAMP)
             den_re[b, rows, :] = den * inverse
             den_im[b, rows, :] = DAMP * inverse
+
+    pl.semaphore_wait(barrier, len(greeted) + len(everyone))
+    for device in mirrors:
+        remote(picked, dip.at[narrow], dip_sems.at[1], device).start()
+    for device in beside:
+        remote(picked, dip.at[narrow], dip_sems.at[0], device).start()
+    loads[2].start()
+    dip[narrow] = picked[...]
+
     loads[0].wait()
 
     def split_rows(i, _):
@@ -157,10 +154,8 @@
         strip = coup[rows, :]
         high, low = halves(strip)
         start = rows_total + i * STRIP
-        for b in range(BLOCKS):
-            cols, there = slice(b * LANES, (b + 1) * LANES), slice(spot(b) * LANES, (spot(b) + 1) * LANES)
-            right[pl.ds(pl.multiple_of(start, STRIP), STRIP), there] = high[:, cols]
-            right[pl.ds(pl.multiple_of(start + virt_total, STRIP), STRIP), there] = low[:, cols]
+        right[pl.ds(pl.multiple_of(start, STRIP), STRIP), :] = high
+        right[pl.ds(pl.multiple_of(start + virt_total, STRIP), STRIP), :] = low
         high, low = high.T, low.T
         for b in range(BLOCKS):
             cols, there = slice(b * LANES, (b + 1) * LANES), (b % 2) * 2 * HALF_COLS + (b // 2) * LANES
@@ -179,8 +174,6 @@
         return 0
 
     lax.fori_loop(0, slab.shape[0] // STRIP, turn_rows, 0)
-    for load in loads[2:]:
-        load.wait()
     same = remote(dip.at[pl.ds(0, NX - 1)], dip.at[pl.ds(0, NX - 1)], dip_sems.at[0], sibling)
     mirrored = remote(dip.at[pl.ds(0, NX)], dip.at[pl.ds(0, NX)], dip_sems.at[1], sibling)
 
@@ -249,8 +242,11 @@
 
     def fold(sweep):
         def share_of(side, strip):
-            cols = pl.ds(pl.multiple_of(side * HALF_COLS + strip * STRIP, STRIP), STRIP)
-            return joined(nn(jnp.concatenate([left[...], left[:, rows_total:]], 1), right[:, cols]))
+            columns_of = [
+                right[:, pl.ds(pl.multiple_of((4 * strip + 2 * i + side) * LANES, LANES), LANES)] for i in range(2)
+            ]
+            rows_of = jnp.concatenate([left[...], left[:, rows_total:]], 1)
+            return joined(nn(rows_of, jnp.concatenate(columns_of, 1)))
 
         swaps = []
         for turn, strip in enumerate(strips):
@@ -315,6 +311,7 @@
     start_half(1 - z_hi)
     doubles_1, singles_1 = expand(1 - z_hi)
     finish(doubles_0 + doubles_1, singles_0 + singles_1)
+    loads[2].wait()
     fold(0)
     for g in range(GROUPS):
         rows, re_rows, im_rows = pl.ds(g * SUB, SUB), pl.ds(g * PIECE, SUB), pl.ds(g * PIECE + SUB, SUB)
@@ -446,7 +443,7 @@
             pltpu.VMEM((BLOCKS * GROUPS, 1, LANES), F32),
             pltpu.VMEM((1, LANES), F32),
             dma((7,)),
-            dma((2 + BLOCKS,)),
+            dma((3,)),
             dma((2, 2)),
             dma((2, 2, 2)),
             dma((2, 2)),

time: 53.1 us -> 52.8 us (level)
  no operation moved by 1% of the time
where the time goes in v6:
time: 52.8 us; the launch traced here: 52.7 us
  Pallas kernels  52.1 us (99%)
  between operations  0.64 us (1%)
    pallas_call x1, Pallas kernels, per_device(): pl.pallas_call(kernel, name='response', out_shape=tuple((pltpu.VMEM(shape...  51.4 us

profile of v6, /device:TPU:1, one launch (start us, length us, event | category | flops | bytes accessed | tf_op | source)
XLA Modules:
  0.0 52.7 jit_solution(2508484732990779782)
XLA Ops:
  0.6 51.4 %response.1 = (f32[2,32,128]{2,1,0:T(8,128)S(1)}, f32[2,32]{1,0:T(2,128)S(1)}) custom-call(s32[256]{0:T(256)} %pair_of_block_hbm.1, f32[256]{0:T(256)} %pair_shift_hbm.1, f32[64]{0:T(128)} %core_energy_hbm.1, s32[2]{0:T(128)} %core_index_hbm.1, f32[16]{0:T(128)} %frequency_hbm.1, f32[8,128]{1,0:T(8,128)} %bitcast.1, f32[64,128]{1,0:T(8,128)} %dipole_hbm.1, ...), custom_call_target="tpu_custom_call" | custom-call | tf_op jit(solution)/shard_map/response/pallas_call | solution.py:404
  52.1 0.6 %tail.1 = (f32[2,32,128]{2,1,0:T(8,128)}, f32[2,32]{1,0:T(2,128)}) custom-call(f32[2,32,128]{2,1,0:T(8,128)S(1)} %get-tuple-element.4.response_in, f32[2,32]{1,0:T(2,128)S(1)} %get-tuple-element.5.rms_in), custom_call_target="tpu_custom_call" | custom-call | tf_op jit(solution)/shard_map/tail/pallas_call | solution.py:463

commit v7 on v6

--- a/solution.py
+++ b/solution.py
@@ -237,8 +237,6 @@
         left[COLS:, :rows_total] = low
 
     parity, far = lax.rem(x, 2), 1 - x // 2
-    strips = (far, 1 - far)
-    reach = ((2 * far + parity, 2 * far + 1 - parity), (3 - 2 * far - parity, 2 - 2 * far + parity))
 
     def fold(sweep):
         def share_of(side, strip):
@@ -248,28 +246,41 @@
             rows_of = jnp.concatenate([left[...], left[:, rows_total:]], 1)
             return joined(nn(rows_of, jnp.concatenate(columns_of, 1)))
 
-        swaps = []
-        for turn, strip in enumerate(strips):
-            share = share_of(1 - core, strip)
+        def swap_of(turn):
+            return remote(part.at[sweep, turn], from_core.at[sweep, turn], core_sems.at[sweep, turn], sibling)
+
+        def give(turn, _):
+            share = share_of(1 - core, lax.rem(far + turn, 2))
             for i in range(2):
                 part[sweep, turn, i] = share[:, i * LANES : (i + 1) * LANES]
-            swap = remote(part.at[sweep, turn], from_core.at[sweep, turn], core_sems.at[sweep, turn], sibling)
-            swap.start()
-            swaps.append(swap)
-        slot = 0
-        for turn, strip in enumerate(strips):
+            swap_of(turn).start()
+            return 0
+
+        def keep(turn, _):
+            strip = lax.rem(far + turn, 2)
             share = share_of(core, strip)
-            swaps[turn].wait_recv()
+            swap_of(turn).wait_recv()
             for i in range(2):
                 own[sweep, 2 * strip + i] = share[:, i * LANES : (i + 1) * LANES] + from_core[sweep, turn, i]
-            for to_x in reach[turn]:
-                for dy in ALONG[: NY if slot < 3 * NY else NY - 1]:
-                    to_y = lax.rem(y + dy, NY)
+            for i in range(2):
+                to_x = 2 * strip + lax.rem(parity + i + turn, 2)
+
+                def send(at):
+                    to_y = lax.rem(y + ALONG[at], NY)
                     remote(
-                        own.at[sweep, to_x, pl.ds(to_y * PIECE, PIECE)], from_plane.at[sweep, slot],
+                        own.at[sweep, to_x, pl.ds(to_y * PIECE, PIECE)],
+                        from_plane.at[sweep, (2 * turn + i) * NY + at],
                         plane_sems.at[sweep], place(to_x, to_y, z, core),
                     ).start()
-                    slot += 1
+
+                for at in range(NY - 1):
+                    send(at)
+                pl.when(turn + i < 2)(lambda: send(NY - 1))
+            return 0
+
+        lax.fori_loop(0, 2, give, 0)
+        lax.fori_loop(0, 2, keep, 0)
+
     def wait_send(ref, sems):
         remote(ref, ref, sems, sibling).wait_send()
 

time: 52.8 us -> 53.1 us (level)
  no operation moved by 1% of the time
where the time goes in v7:
time: 53.1 us; the launch traced here: 53 us
  Pallas kernels  52.3 us (98%)
  between operations  0.64 us (1%)
    pallas_call x1, Pallas kernels, per_device(): pl.pallas_call(kernel, name='response', out_shape=tuple((pltpu.VMEM(shape...  51.7 us

profile of v7, /device:TPU:1, one launch (start us, length us, event | category | flops | bytes accessed | tf_op | source)
XLA Modules:
  0.0 53.0 jit_solution(805472288625468646)
XLA Ops:
  0.6 51.7 %response.1 = (f32[2,32,128]{2,1,0:T(8,128)S(1)}, f32[2,32]{1,0:T(2,128)S(1)}) custom-call(s32[256]{0:T(256)} %pair_of_block_hbm.1, f32[256]{0:T(256)} %pair_shift_hbm.1, f32[64]{0:T(128)} %core_energy_hbm.1, s32[2]{0:T(128)} %core_index_hbm.1, f32[16]{0:T(128)} %frequency_hbm.1, f32[8,128]{1,0:T(8,128)} %bitcast.1, f32[64,128]{1,0:T(8,128)} %dipole_hbm.1, ...), custom_call_target="tpu_custom_call" | custom-call | tf_op jit(solution)/shard_map/response/pallas_call | solution.py:415
  52.4 0.6 %tail.1 = (f32[2,32,128]{2,1,0:T(8,128)}, f32[2,32]{1,0:T(2,128)}) custom-call(f32[2,32,128]{2,1,0:T(8,128)S(1)} %get-tuple-element.4.response_in, f32[2,32]{1,0:T(2,128)S(1)} %get-tuple-element.5.rms_in), custom_call_target="tpu_custom_call" | custom-call | tf_op jit(solution)/shard_map/tail/pallas_call | solution.py:474

commit v8 on v6

--- a/solution.py
+++ b/solution.py
@@ -70,7 +70,7 @@
     picked, dip, rhs, pre_re, pre_im, level, den_re, den_im, resp, base, res,
     pieces, left,
     part, from_core, own, from_plane, columns, applied, final, lines, line_out,
-    small_sem, hbm_sem, dip_sems, core_sems, plane_sems, column_sems, gather_sems, share_sem,
+    small_sem, hbm_sem, dip_sems, core_sems, plane_sems, column_sems, gather_sems, share_sems,
     final_sems, line_sems,
 ):
     wide, narrow = lax.axis_index("wide"), lax.axis_index("narrow")
@@ -191,23 +191,22 @@
                 pieces[half, g * PIECE : (g + 1) * PIECE, cols] = high
                 pieces[half, COLS + g * PIECE : COLS + (g + 1) * PIECE, cols] = low
 
-    def next_half(half):
+    def next_block(half, j):
+        b, cols = half * HALF + j, pl.ds(pl.multiple_of(j * LANES, LANES), LANES)
         for g in range(GROUPS):
             rows, re_rows, im_rows = pl.ds(g * SUB, SUB), pl.ds(g * PIECE, SUB), pl.ds(g * PIECE + SUB, SUB)
-            for j in range(HALF):
-                b, cols = half * HALF + j, slice(j * LANES, (j + 1) * LANES)
-                res_re = base[b, re_rows, :] - applied[b, re_rows, :]
-                res_im = base[b, im_rows, :] - applied[b, im_rows, :]
-                res[b, re_rows, :] = res_re
-                res[b, im_rows, :] = res_im
-                p_re, p_im = pre_re[b, rows, :], pre_im[b, rows, :]
-                re = resp[0, b, re_rows, :] + (res_re * p_re - res_im * p_im)
-                im = resp[0, b, im_rows, :] + (res_im * p_re + res_re * p_im)
-                resp[1, b, re_rows, :] = re
-                resp[1, b, im_rows, :] = im
-                high, low = halves(jnp.concatenate([re, im], 0))
-                pieces[half, g * PIECE : (g + 1) * PIECE, cols] = high
-                pieces[half, COLS + g * PIECE : COLS + (g + 1) * PIECE, cols] = low
+            res_re = base[b, re_rows, :] - applied[b, re_rows, :]
+            res_im = base[b, im_rows, :] - applied[b, im_rows, :]
+            res[b, re_rows, :] = res_re
+            res[b, im_rows, :] = res_im
+            p_re, p_im = pre_re[b, rows, :], pre_im[b, rows, :]
+            re = resp[0, b, re_rows, :] + (res_re * p_re - res_im * p_im)
+            im = resp[0, b, im_rows, :] + (res_im * p_re + res_re * p_im)
+            resp[1, b, re_rows, :] = re
+            resp[1, b, im_rows, :] = im
+            high, low = halves(jnp.concatenate([re, im], 0))
+            pieces[half, g * PIECE : (g + 1) * PIECE, cols] = high
+            pieces[half, COLS + g * PIECE : COLS + (g + 1) * PIECE, cols] = low
 
     def joined(both):
         return both[:COLS] + both[COLS:]
@@ -322,17 +321,31 @@
     total = collect(0)
     block = applied.at[core * HALF + x, pl.ds(y * PIECE, PIECE)]
     applied[core * HALF + x, pl.ds(y * PIECE, PIECE), :] = total
-    for device in plane:
-        remote(block, block, gather_sems, device).start()
-    slots = from_plane.at[0]
-    remote(slots, slots, gather_sems, sibling).wait_recv()
-    mine = applied.at[pl.ds(core * HALF, HALF)]
-    share = remote(mine, mine, share_sem, sibling)
-    share.start()
-    next_half(core)
+    for (dx, _), device in zip(PLANE, plane):
+        remote(block, block, gather_sems.at[int(dx == 2)], device).start()
+    across_x = [lax.rem(x + d, NX) for d in (0, 1, 3, 2)]
+
+    def pass_on(j, sems):
+        mine = applied.at[core * HALF + j]
+        remote(mine, mine, sems, sibling).start()
+
+    near_slots = from_plane.at[0, pl.ds(0, len(plane) - NY)]
+    far_slots = from_plane.at[0, pl.ds(0, NY)]
+    remote(near_slots, near_slots, gather_sems.at[0], sibling).wait_recv()
+    for j in across_x[:3]:
+        pass_on(j, share_sems.at[0])
+    for j in across_x[:3]:
+        next_block(core, j)
+    remote(far_slots, far_slots, gather_sems.at[1], sibling).wait_recv()
+    pass_on(across_x[3], share_sems.at[1])
+    next_block(core, across_x[3])
     doubles_0, singles_0 = expand(core)
-    share.wait_recv()
-    next_half(1 - core)
+    three, one = applied.at[pl.ds(0, 3)], applied.at[pl.ds(0, 1)]
+    remote(three, three, share_sems.at[0], sibling).wait_recv()
+    for j in across_x[:3]:
+        next_block(1 - core, j)
+    remote(one, one, share_sems.at[1], sibling).wait_recv()
+    next_block(1 - core, across_x[3])
     doubles_1, singles_1 = expand(1 - core)
     finish(doubles_0 + doubles_1, singles_0 + singles_1)
     fold(1)
@@ -374,8 +387,10 @@
     wait_send(seven, final_sems)
 
     wait_dipoles()
-    share.wait_send()
-    wait_send(from_plane.at[0], gather_sems)
+    wait_send(near_slots, gather_sems.at[0])
+    wait_send(far_slots, gather_sems.at[1])
+    wait_send(three, share_sems.at[0])
+    wait_send(one, share_sems.at[1])
     for sweep in range(2):
         wait_swaps(sweep)
         wait_send(from_plane.at[sweep], plane_sems.at[sweep])
@@ -448,8 +463,8 @@
             dma((2, 2, 2)),
             dma((2, 2)),
             dma((2, 2)),
-            dma((2,)),
-            dma((2,)),
+            dma((2, 2)),
+            dma((2, 2)),
             dma((2,)),
             dma((2,)),
         ],

time: 52.8 us -> 52.9 us (level)
  no operation moved by 1% of the time
where the time goes in v8:
time: 52.9 us; the launch traced here: 52.8 us
  Pallas kernels  52.1 us (98%)
  between operations  0.64 us (1%)
    pallas_call x1, Pallas kernels, per_device(): pl.pallas_call(kernel, name='response', out_shape=tuple((pltpu.VMEM(shape...  51.5 us

profile of v8, /device:TPU:1, one launch (start us, length us, event | category | flops | bytes accessed | tf_op | source)
XLA Modules:
  0.0 52.8 jit_solution(17112829155316277556)
XLA Ops:
  0.6 51.5 %response.1 = (f32[2,32,128]{2,1,0:T(8,128)S(1)}, f32[2,32]{1,0:T(2,128)S(1)}) custom-call(s32[256]{0:T(256)} %pair_of_block_hbm.1, f32[256]{0:T(256)} %pair_shift_hbm.1, f32[64]{0:T(128)} %core_energy_hbm.1, s32[2]{0:T(128)} %core_index_hbm.1, f32[16]{0:T(128)} %frequency_hbm.1, f32[8,128]{1,0:T(8,128)} %bitcast.1, f32[64,128]{1,0:T(8,128)} %dipole_hbm.1, ...), custom_call_target="tpu_custom_call" | custom-call | tf_op jit(solution)/shard_map/response/pallas_call | solution.py:419
  52.2 0.6 %tail.1 = (f32[2,32,128]{2,1,0:T(8,128)}, f32[2,32]{1,0:T(2,128)}) custom-call(f32[2,32,128]{2,1,0:T(8,128)S(1)} %get-tuple-element.4.response_in, f32[2,32]{1,0:T(2,128)S(1)} %get-tuple-element.5.rms_in), custom_call_target="tpu_custom_call" | custom-call | tf_op jit(solution)/shard_map/tail/pallas_call | solution.py:478

commit v9 on v6

--- a/solution.py
+++ b/solution.py
@@ -362,16 +362,24 @@
     final[core, 1, rows, :] = im + (res_im * p_re + res_re * p_im)
     block = final.at[core, :, rows]
     near = [place(x, lax.rem(y + d, NY), z, c) for d in ALONG[:-1] for c in (1 - core, core)]
-    for device in near + [sibling]:
-        remote(block, block, final_sems, device).start()
-    seven = columns.at[1, pl.ds(0, NZ - 1)]
-    remote(seven, seven, final_sems, sibling).wait_recv()
+
+    def show():
+        for device in near + [sibling]:
+            remote(block, block, final_sems, device).start()
+
+    def await_pieces(count):
+        pieces_in = columns.at[1, pl.ds(0, count)]
+        remote(pieces_in, pieces_in, final_sems, sibling).wait_recv()
+
+    pl.when(core == z_hi)(show)
+    pl.when(core == z_hi)(lambda: await_pieces(NY - 1))
+    pl.when(core != z_hi)(lambda: await_pieces(NY))
     out_ref[...] = final[z_hi]
     most = lines.at[pl.ds(0, BLOCKS * GROUPS - 1)]
     remote(most, most, line_sems, sibling).wait_recv()
     rms_ref[1:2, :] = rms_of(jnp.sum(lines[...], axis=0))
     wait_send(most, line_sems)
-    wait_send(seven, final_sems)
+    pl.when(core == z_hi)(lambda: wait_send(columns.at[1, pl.ds(0, NZ - 1)], final_sems))
 
     wait_dipoles()
     share.wait_send()

time: 52.8 us -> 52.7 us (level)
  no operation moved by 1% of the time
where the time goes in v9:
time: 52.7 us; the launch traced here: 52.6 us
  Pallas kernels  51.9 us (98%)
  between operations  0.64 us (1%)
    pallas_call x1, Pallas kernels, per_device(): pl.pallas_call(kernel, name='response', out_shape=tuple((pltpu.VMEM(shape...  51.3 us

profile of v9, /device:TPU:1, one launch (start us, length us, event | category | flops | bytes accessed | tf_op | source)
XLA Modules:
  0.0 52.6 jit_solution(13619628289027441388)
XLA Ops:
  0.6 51.3 %response.1 = (f32[2,32,128]{2,1,0:T(8,128)S(1)}, f32[2,32]{1,0:T(2,128)S(1)}) custom-call(s32[256]{0:T(256)} %pair_of_block_hbm.1, f32[256]{0:T(256)} %pair_shift_hbm.1, f32[64]{0:T(128)} %core_energy_hbm.1, s32[2]{0:T(128)} %core_index_hbm.1, f32[16]{0:T(128)} %frequency_hbm.1, f32[8,128]{1,0:T(8,128)} %bitcast.1, f32[64,128]{1,0:T(8,128)} %dipole_hbm.1, ...), custom_call_target="tpu_custom_call" | custom-call | tf_op jit(solution)/shard_map/response/pallas_call | solution.py:412
  52.0 0.6 %tail.1 = (f32[2,32,128]{2,1,0:T(8,128)}, f32[2,32]{1,0:T(2,128)}) custom-call(f32[2,32,128]{2,1,0:T(8,128)S(1)} %get-tuple-element.4.response_in, f32[2,32]{1,0:T(2,128)S(1)} %get-tuple-element.5.rms_in), custom_call_target="tpu_custom_call" | custom-call | tf_op jit(solution)/shard_map/tail/pallas_call | solution.py:471
